TPU v7x, 32 devices: a whole 2x2x4 slice. The times are simulated.
32 devices in a mesh: atm: 8 (over z, y), cpl: 4 (over x, core).
Axes of the slice: x: 2, y: 2, z: 4, core: 2. Of those that a mesh axis runs over, the one named last changes fastest.
Arguments:
- air_temp: float32 [192, 64, 512], P('atm', None, 'cpl'), may hold values from -6 to 6
- wind_field: bfloat16 [2, 192, 64, 512], P(None, 'atm', None, 'cpl'), may hold values from -0.3984375 to 0.3984375
- physics: float32 [64, 64], replicated, may hold values from -0.75 to 0.75
- sea_surface: float32 [192, 512], P('atm', 'cpl'), may hold values from -6 to 6
- shortwave: float32 [192, 512], P('atm', 'cpl'), may hold values from 0 to 1
- ocean_mask: int32 [192, 512], P('atm', 'cpl'), may hold values 0 or 1
- owner_route: int32 [4, 192, 1], P('cpl', 'atm'), may hold values from 0 to 3; in each aligned block of 24 rows (0 to 23, 24 to 47, ..., all dimensions but the last counted through in order) at most 12 rows name the same one
- ocean_tile: int32 [4, 192], P('cpl', 'atm'), may hold values from 0 to 23
- weight_tile: int32 [4, 192], P('cpl', 'atm'), may hold values from 0 to 15
- remap_tiles: float32 [16, 32, 128], replicated, may hold values from 0.002 to 0.03
- ocean_temp: float32 [80, 24576], P(None, ('atm', 'cpl')), may hold values from -6 to 6
- mixing: float32 [80, 80], replicated, may hold values from -0.625 to 0.625
Outputs:
- air_next: float32 [192, 64, 512], P('atm', None, 'cpl')
- ocean_next: float32 [80, 24576], P(None, ('atm', 'cpl'))
- surface_temp: float32 [192, 512], P('atm', 'cpl')
Inputs may be any that keep to these rules, and one draw needn't show every extreme that they name: `owner_route`: among the 24 tiles of one device at most 12 name the same owner, and in every draw some device's tiles name one owner exactly 12 times. `ocean_tile`: ocean tile index within the owner. `weight_tile`: row of remap_tiles used by the tile.
All inputs are finite; a program needn't handle non-finite values. No bound on the sum of `ocean_mask` on one device may be relied on, other than what follows from the above.
Results may differ from a plain program's by a relative error of at most 0.0015.
Values may be sent and summed in bfloat16 or wider, within the bound.
No kernel may reach another device: no remote copies, remote signals or barrier semaphores. Data moves between devices by JAX's collectives and lax.ppermute only.
A program may use at most 64 MiB of HBM per device.

v0:
```python
import jax
import jax.numpy as jnp
from jax import lax
from jax.experimental import pallas as pl
from jax.experimental.pallas import tpu as pltpu
from jax.sharding import PartitionSpec as P

diffusion_rate = 0.05
physics_rate = 0.5
highest = lax.Precision.HIGHEST
f32 = jnp.float32
bf16 = jnp.bfloat16


def pair_even(count):
    return [(i, i ^ 1) for i in range(count)]


def pair_odd(count):
    up = [(i, (i + 1) % count) for i in range(1, count, 2)]
    return up + [(target, source) for source, target in up]


def exchange(block, axis):
    count = lax.axis_size(axis)
    odd_side = lax.ppermute(block, axis, pair_odd(count))
    even_side = lax.ppermute(block, axis, pair_even(count))
    return even_side, odd_side


def shift(block, axis, turn):
    count = lax.axis_size(axis)
    return lax.ppermute(block, axis, [(i, (i + turn) % count) for i in range(count)])


def iota(shape, dim):
    return lax.broadcasted_iota(jnp.int32, shape, dim)


def roll(value, shift):
    return pltpu.roll(value, shift % value.shape[-1], value.ndim - 1)


def pick(flag, yes, no):
    return jnp.where(flag, yes, no)


def rates(first, second):
    return (
        jnp.maximum(first, 0.0) + diffusion_rate,
        diffusion_rate - jnp.minimum(first, 0.0),
        jnp.maximum(second, 0.0) + diffusion_rate,
        diffusion_rate - jnp.minimum(second, 0.0),
    )


def split(value):
    high = value.astype(bf16)
    return high, (value - high.astype(f32)).astype(bf16)


def physics_stack(physics):
    high, low = split(physics)
    return jnp.concatenate([high, high, low], axis=1)


def column(stack, field):
    high, low = split(field)
    tendency = jnp.dot(
        stack, jnp.concatenate([high, low, high], axis=0), preferred_element_type=f32
    )
    return field + physics_rate * jnp.tanh(tendency)


def pack_kernel(air, wind, *refs):
    others = (len(refs) - 5) // 2
    packed, air_here, wind_here = refs[others : others + 3]
    sems, other_sems = refs[-2:]
    rows, levels, width = air.shape
    lane = iota((levels, width), 1)
    place = lane // 4
    kind = lane % 4
    parts = sems.shape[1]
    size = rows // parts
    copies = []
    for part in range(parts):
        span = pl.ds(part * size, size)
        copies.append(
            (
                pltpu.make_async_copy(air.at[span], air_here.at[span], sems.at[0, part]),
                pltpu.make_async_copy(wind.at[:, span], wind_here.at[:, span], sems.at[1, part]),
            )
        )
        for copy in copies[-1]:
            copy.start()
    later = [
        pltpu.make_async_copy(source, target, other_sems.at[at])
        for at, (source, target) in enumerate(zip(refs[:others], refs[others + 3 : -2]))
    ]
    for copy in later:
        copy.start()
    cells = jnp.zeros((levels, width), f32)
    first = jnp.zeros((levels, width), f32)
    second = jnp.zeros((levels, width), f32)
    for x in range(rows):
        if x % size == 0:
            for copy in copies[x // size]:
                copy.wait()
        here = place == x
        cells = pick(here, roll(air_here[x], 4 * x + 2), cells)
        first = pick(here, roll(wind_here[0, x].astype(f32), 4 * x + 2), first)
        second = pick(here, roll(wind_here[1, x].astype(f32), 4 * x + 2), second)
    winds = pick((kind == 1) | (kind == 2), first, roll(second, 2))
    packed[0] = cells.astype(bf16)
    packed[1] = winds.astype(bf16)
    for copy in later:
        copy.wait()


def cpl_sides(even_side, odd_side):
    upper = lax.axis_index("cpl") % 2 == 0
    high = pick(upper, even_side[...].astype(f32), odd_side[...].astype(f32))
    low = pick(upper, odd_side[...].astype(f32), even_side[...].astype(f32))
    return low, high


def outer_cells(low, high):
    kind = iota(low.shape[1:], 1) % 4
    return pick(kind < 2, low[0], high[0])


def swap_cells(cells):
    kind = iota(cells.shape, 1) % 4
    return pick(kind == 2, roll(cells, 1), roll(cells, -1))


def sideways(field, swapped, x):
    width = field.shape[1]
    lane = iota(field.shape, 1)
    halo = roll(swapped, -(4 * x + 2))
    south = pick(lane == 0, halo, roll(field, 1))
    north = pick(lane == width - 1, halo, roll(field, -1))
    return south, north


def advance_row(center, west, east, south, north, speeds):
    cw, ce, cs, cn = speeds
    return (
        center
        + (cw * (west - center) + ce * (east - center))
        + (cs * (south - center) + cn * (north - center))
    )


def advance_outer(own, low, high, outer, west, east):
    kind = iota(outer.shape, 1) % 4
    south = roll(pick(kind == 0, outer, own), 1)
    north = roll(pick(kind == 3, outer, own), -1)
    first = pick(kind == 1, low[1], high[1])
    second = roll(pick(kind == 3, low[1], high[1]), -2)
    return advance_row(outer, west, east, south, north, rates(first, second))


def make_edge_kernel(rows, upper):
    def edge_kernel(air, wind, even_side, odd_side, _, message, partial):
        low, high = cpl_sides(even_side, odd_side)
        outer = outer_cells(low, high)
        center, inner = (air[1], air[0]) if upper else (air[0], air[1])
        cw, ce, cs, cn = rates(wind[0, 0].astype(f32), wind[1, 0].astype(f32))
        inside, outside = (cw, ce) if upper else (ce, cw)
        south, north = sideways(center, swap_cells(outer), rows - 1 if upper else 0)
        known = (
            center
            + (inside * (inner - center) - outside * center)
            + (cs * (south - center) + cn * (north - center))
        )
        partial[0] = known
        partial[1] = outside
        for at, value in enumerate((center, known, outside, outer)):
            message[at] = value.astype(bf16)

    return edge_kernel


def inner_kernel(
    air, wind, physics, own, even_side, odd_side, air_next, near, bottom, field, ready, sems
):
    rows, levels, width = air.shape
    low, high = cpl_sides(even_side, odd_side)
    outer = outer_cells(low, high)
    stack = physics_stack(physics[...])
    swapped = swap_cells(outer)
    after = advance_outer(
        own[0].astype(f32), low, high, outer, roll(outer, 4), roll(outer, -4)
    )
    swapped_after = swap_cells(column(stack, after))

    def speeds(x):
        return rates(wind[0, x].astype(f32), wind[1, x].astype(f32))

    def step(source, halo, x):
        center = source[x]
        south, north = sideways(center, halo, x)
        return advance_row(center, source[x - 1], source[x + 1], south, north, speeds(x))

    def pair(source, halo, x):
        return column(stack, jnp.concatenate([step(source, halo, x), step(source, halo, x + 1)], axis=1))

    for x in range(1, rows - 1, 2):
        both = pair(air, swapped, x)
        field[x] = both[:, :width]
        field[x + 1] = both[:, width:]
    near[0] = field[1]
    near[1] = field[2]
    near[2] = field[rows - 3]
    near[3] = field[rows - 2]
    bottom[...] = jnp.zeros_like(bottom)
    copies = []
    for x in range(2, rows - 2, 2):
        both = pair(field, swapped_after, x)
        ready[x] = both[:, :width]
        ready[x + 1] = both[:, width:]
        bottom[x : x + 1] = both[0:1, :width]
        bottom[x + 1 : x + 2] = both[0:1, width:]
        span = pl.ds(x, 2)
        copies.append(pltpu.make_async_copy(ready.at[span], air_next.at[span], sems.at[x // 2 - 1]))
        copies[-1].start()
    for copy in copies:
        copy.wait()


def as_column(row):
    size = row.shape[1]
    square = jnp.broadcast_to(row, (size, size))
    return jnp.sum(
        jnp.where(iota((size, size), 0) == iota((size, size), 1), square, 0.0),
        axis=1,
        keepdims=True,
    )


def fold(value, size):
    span = value.shape[1] // 2
    while span >= size:
        value = value + roll(value, span)
        span //= 2
    return value


def chosen_shares(fluxes, weights, bank, ocean_width):
    rows, width = fluxes.shape
    every = lax.dot_general(
        fluxes, weights, (((1,), (1,)), ((), ())), precision=highest, preferred_element_type=f32
    )
    total = jnp.zeros((rows, width), f32)
    for at in range(0, weights.shape[0], width):
        block = (iota((rows, width), 1) + at) // ocean_width
        total = total + jnp.where(block == bank, every[:, at : at + width], 0.0)
    return fold(total, ocean_width)


def start_kernel(
    winds, shortwave, mask, route, tile, bank, weights, ocean, mixing, _,
    exchange_rate, total_weight, message, base, response,
):
    rows, width = shortwave.shape
    depth = ocean.shape[0]
    banks, ocean_width, _ = weights.shape
    flat = weights[...].reshape(banks * ocean_width, width)
    frac = mask[...].astype(f32)
    bank_at = as_column(bank[...].astype(f32)).astype(jnp.int32)
    for x in range(rows):
        first = winds[0, x].astype(f32)[0:1]
        second = winds[1, x].astype(f32)[0:1]
        exchange_rate[x : x + 1] = first * first + second * second
    exchange_rate[...] = frac * (0.5 + 2.0 * jnp.sqrt(exchange_rate[...] + 0.01))
    solar = chosen_shares(frac * shortwave[...], flat, bank_at, ocean_width)
    lane = iota((rows, width), 1)
    total = jnp.zeros((rows, width), f32)
    for at in range(0, banks * ocean_width, width):
        hot = ((lane + at) // ocean_width == bank_at).astype(f32)
        total = total + jnp.dot(hot, flat[at : at + width], precision=highest, preferred_element_type=f32)
    total_weight[...] = total

    held = ocean[...]
    mixed = mixing[...]
    settled = 0.5 * held + jnp.dot(mixed, held, precision=highest, preferred_element_type=f32)
    base[...] = settled
    level = iota((depth, width), 0)
    profile = jnp.exp(level.astype(f32) / -8.0)
    profile = profile / jnp.sum(profile, axis=0, keepdims=True)
    part = iota((depth, width), 1)
    unit = jnp.where(part == 0, (level == 0).astype(f32), jnp.where(part == 1, profile, 0.0))
    response[...] = 0.5 * unit + jnp.dot(mixed, unit, precision=highest, preferred_element_type=f32)

    group = lax.axis_index("cpl")
    surface = jnp.zeros((rows, width), f32)
    for at in range(0, rows * ocean_width, width):
        spread = jnp.broadcast_to(settled[0:1, at : at + width], (rows, width))
        surface = surface + jnp.where((lane + at) // ocean_width == iota((rows, width), 0), spread, 0.0)
    surface = fold(surface, ocean_width)
    target = route[...] * rows + tile[...]
    target_at = as_column(target.astype(f32))
    own_at = (group * rows + iota((rows, width), 0)).astype(f32)
    message[...] = jnp.full(message.shape, -1.0, f32)
    message[0:rows, :] = jnp.where(
        lane < 2 * ocean_width,
        solar,
        jnp.where(
            lane < 3 * ocean_width,
            surface,
            jnp.where(lane == 3 * ocean_width, target_at, own_at),
        ),
    )
    message[rows : rows + 1, 0:rows] = target.astype(f32)
    message[rows : rows + 1, ocean_width : ocean_width + rows] = (
        group * rows + iota((1, rows), 1)
    ).astype(f32)


def make_outer_kernel(rows):
    def outer_kernel(
        above_ref, below_ref, partial_low, partial_high, air_low, air_high, wind_low, wind_high, own, even_side, odd_side,
        near, physics, bottom, rate, sea, bank, weights, start,
        air_edges, bottom_next, message,
    ):
        width = sea.shape[1]
        banks, ocean_width, _ = weights.shape
        above = above_ref[...].astype(f32)
        below = below_ref[...].astype(f32)
        low, high = cpl_sides(even_side, odd_side)
        outer = outer_cells(low, high)
        stack = physics_stack(physics[...])
        place = iota(outer.shape, 1) // 4
        after = advance_outer(
            own[0].astype(f32),
            low,
            high,
            outer,
            pick(place == 0, roll(below[3], -4 * (rows - 1)), roll(outer, 4)),
            pick(place == rows - 1, roll(above[3], 4 * (rows - 1)), roll(outer, -4)),
        )
        moved = jnp.concatenate(
            [
                below[1] + below[2] * air_low[0],
                partial_low[0] + partial_low[1] * below[0],
                partial_high[0] + partial_high[1] * above[0],
                above[1] + above[2] * air_high[1],
                after,
            ],
            axis=1,
        )
        stepped = column(stack, moved)
        parts = [stepped[:, at * width : (at + 1) * width] for at in range(5)]
        halo = swap_cells(parts[4])
        inner = [near[at] for at in range(4)]
        bottom_next[...] = bottom[...]
        cells = []
        for center, west, east, wind, at, x in (
            (parts[1], parts[0], inner[0], wind_low, 0, 0),
            (inner[0], parts[1], inner[1], wind_low, 1, 1),
            (inner[3], inner[2], parts[2], wind_high, 0, rows - 2),
            (parts[2], inner[3], parts[3], wind_high, 1, rows - 1),
        ):
            south, north = sideways(center, halo, x)
            speeds = rates(wind[0, at].astype(f32), wind[1, at].astype(f32))
            cells.append(advance_row(center, west, east, south, north, speeds))
        final = column(stack, jnp.concatenate(cells, axis=1))
        for at, x in enumerate((0, 1, rows - 2, rows - 1)):
            row = final[:, at * width : (at + 1) * width]
            air_edges[at] = row
            bottom_next[x : x + 1] = row[0:1]
        heat = rate[...] * (bottom_next[...] - sea[...])
        flat = weights[...].reshape(banks * ocean_width, width)
        bank_at = as_column(bank[...].astype(f32)).astype(jnp.int32)
        shares = chosen_shares(heat, flat, bank_at, ocean_width)
        message[...] = start[...]
        message[0:rows, :] = jnp.where(
            iota((rows, width), 1) < ocean_width, shares, start[0:rows, :]
        )

    return outer_kernel


def patch_kernel(edges, _, out, sems):
    rows = out.shape[0]
    copies = [
        pltpu.make_async_copy(edges.at[pl.ds(0, 2)], out.at[pl.ds(0, 2)], sems.at[0]),
        pltpu.make_async_copy(edges.at[pl.ds(2, 2)], out.at[pl.ds(rows - 2, 2)], sems.at[1]),
    ]
    for copy in copies:
        copy.start()
    for copy in copies:
        copy.wait()


def make_last_kernel(count):
    def last_kernel(*refs):
        messages, (base, response, total_weight, bottom, mask, bank, weights, ocean_next, surface) = (
            refs[:count],
            refs[count:],
        )
        own = messages[0][...]
        if len(messages) == 2 and len(messages[1].shape) == 3:
            blocks = [messages[1][at] for at in range(messages[1].shape[0])]
        else:
            blocks = [ref[...] for ref in messages]
        rows, width = bottom.shape
        banks, ocean_width, _ = weights.shape
        slots = own.shape[0]
        depth = base.shape[0]
        own_part = own[0:rows]
        wanted = jnp.concatenate(
            [
                own_part[:, 3 * ocean_width : 3 * ocean_width + 1],
                own_part[:, 3 * ocean_width + 1 : 3 * ocean_width + 2],
            ],
            axis=0,
        )
        top = response[0:1, 0:1]
        sun = response[0:1, 1:2]
        lane = iota((slots, width), 1)
        hot = []
        values = []
        for block in blocks:
            label = block[rows : rows + 1, 0 : 2 * ocean_width]
            hot.append((wanted == label).astype(f32))
            raised = top * roll(block, 2 * ocean_width) + sun * roll(block, ocean_width)
            values.append(
                jnp.where(
                    lane < 2 * ocean_width, block, jnp.where(lane < 3 * ocean_width, raised, 0.0)
                )
            )
            values.append(
                jnp.where((lane >= 2 * ocean_width) & (lane < 3 * ocean_width), block, 0.0)
            )
        got = jnp.dot(
            jnp.concatenate(hot, axis=1),
            jnp.concatenate(values, axis=0),
            precision=highest,
            preferred_element_type=f32,
        )
        near = iota((rows, width), 1)
        seen = fold(
            jnp.where(
                (near >= 2 * ocean_width) & (near < 3 * ocean_width), got[0:rows], 0.0
            ),
            ocean_width,
        )
        forcing = got[rows : 2 * rows]
        heat = fold(jnp.where(near < ocean_width, forcing, 0.0), ocean_width)
        solar = fold(
            jnp.where((near >= ocean_width) & (near < 2 * ocean_width), forcing, 0.0), ocean_width
        )
        first = response[:, 0:1]
        second = response[:, 1:2]
        for at in range(0, base.shape[1], width):
            mine = (near + at) // ocean_width == iota((rows, width), 0)
            heat_row = jnp.sum(jnp.where(mine, heat, 0.0), axis=0, keepdims=True)
            solar_row = jnp.sum(jnp.where(mine, solar, 0.0), axis=0, keepdims=True)
            ocean_next[:, at : at + width] = base[:, at : at + width] + (
                first * heat_row + second * solar_row
            )
        flat = weights[...].reshape(banks * ocean_width, width)
        bank_at = as_column(bank[...].astype(f32)).astype(jnp.int32)
        spread = jnp.concatenate(
            [
                jnp.where((near + at) // ocean_width == bank_at, seen, 0.0)
                for at in range(0, banks * ocean_width, width)
            ],
            axis=1,
        )
        weighted = jnp.dot(spread, flat, precision=highest, preferred_element_type=f32)
        frac = mask[...].astype(f32)
        surface[...] = frac * (weighted / total_weight[...]) + (1.0 - frac) * bottom[...]

    return last_kernel


def shape_of(shape, dtype=f32):
    return jax.ShapeDtypeStruct(shape, dtype)


def whole(count):
    return [pl.BlockSpec(memory_space=pltpu.VMEM) for _ in range(count)]


def in_hbm(value):
    return pltpu.with_memory_space_constraint(value, pltpu.HBM)


params = pltpu.CompilerParams(vmem_limit_bytes=48 * 1024 * 1024)


def local(
    air_temp,
    wind_field,
    physics,
    sea_surface,
    shortwave,
    ocean_mask,
    owner_route,
    ocean_tile,
    weight_tile,
    remap_tiles,
    ocean_temp,
    mixing,
):
    rows, levels, width = air_temp.shape
    groups = lax.axis_size("cpl")
    ocean_width = remap_tiles.shape[1]
    slots = ocean_width
    ocean_shape = ocean_temp.shape

    others = (
        physics,
        sea_surface,
        shortwave,
        ocean_mask,
        owner_route.reshape(1, rows),
        ocean_tile,
        weight_tile,
        remap_tiles,
        ocean_temp,
        mixing,
    )
    (
        packed,
        air_here,
        wind_here,
        physics,
        sea_surface,
        shortwave,
        ocean_mask,
        owner_route,
        ocean_tile,
        weight_tile,
        remap_tiles,
        ocean_temp,
        mixing,
    ) = (
        pl.pallas_call(
            pack_kernel,
            out_shape=(pltpu.VMEM((2, levels, width), bf16),)
            + tuple(
                pltpu.VMEM(value.shape, value.dtype) for value in (air_temp, wind_field) + others
            ),
            in_specs=[pl.BlockSpec(memory_space=pltpu.HBM)] * (2 + len(others)),
            out_specs=tuple(whole(3 + len(others))),
            scratch_shapes=[
                pltpu.SemaphoreType.DMA((2, 2)),
                pltpu.SemaphoreType.DMA((len(others),)),
            ],
            compiler_params=params,
            name="pack",
        )(*(in_hbm(value) for value in (air_temp, wind_field) + others))
    )
    even_side, odd_side = exchange(packed, "cpl")

    exchange_rate, total_weight, start, base, response = pl.pallas_call(
        start_kernel,
        grid=(1,),
        out_shape=(
            shape_of((rows, width)),
            shape_of((rows, width)),
            shape_of((slots, width)),
            shape_of(ocean_shape),
            shape_of((ocean_shape[0], width)),
        ),
        in_specs=[pl.BlockSpec((2, rows, 16, width), lambda i: (0, 0, 0, 0))]
        + whole(8)
        + [pl.BlockSpec(memory_space=pl.ANY)],
        out_specs=whole(5),
        compiler_params=params,
        name="start",
    )(
        wind_here,
        shortwave,
        ocean_mask,
        owner_route,
        ocean_tile,
        weight_tile,
        remap_tiles,
        ocean_temp,
        mixing,
        packed,
    )

    last_pair = rows // 2 - 1
    air_specs = [
        pl.BlockSpec((2, levels, width), lambda i: (0, 0, 0)),
        pl.BlockSpec((2, levels, width), lambda i: (last_pair, 0, 0)),
    ]

    def edge(upper, after):
        return pl.pallas_call(
            make_edge_kernel(rows, upper),
            grid=(1,),
            out_shape=(shape_of((4, levels, width), bf16), shape_of((2, levels, width))),
            in_specs=[
                air_specs[upper],
                pl.BlockSpec((2, 1, levels, width), lambda i: (0, (rows - 1) * upper, 0, 0)),
            ]
            + whole(2)
            + [pl.BlockSpec(memory_space=pl.ANY)],
            out_specs=whole(2),
            compiler_params=params,
            name="edge",
        )(air_here, wind_here, even_side, odd_side, after)

    to_high, partial_high = edge(1, start)
    below = shift(to_high, "atm", 1)
    to_low, partial_low = edge(0, partial_high)
    above = shift(to_low, "atm", -1)

    air_inner, near, bottom = pl.pallas_call(
        inner_kernel,
        out_shape=(
            shape_of((rows, levels, width)),
            shape_of((4, levels, width)),
            shape_of((rows, width)),
        ),
        in_specs=whole(6),
        out_specs=tuple([pl.BlockSpec(memory_space=pltpu.HBM)] + whole(2)),
        scratch_shapes=[
            pltpu.VMEM((rows, levels, width), f32),
            pltpu.VMEM((rows, levels, width), f32),
            pltpu.SemaphoreType.DMA((rows // 2 - 2,)),
        ],
        compiler_params=params,
        name="inner",
    )(air_here, wind_here, physics, packed, even_side, odd_side)

    air_edges, bottom_next, message = pl.pallas_call(
        make_outer_kernel(rows),
        grid=(1,),
        out_shape=(
            shape_of((4, levels, width)),
            shape_of((rows, width)),
            shape_of((slots, width)),
        ),
        in_specs=whole(4)
        + air_specs
        + [
            pl.BlockSpec((2, 2, levels, width), lambda i: (0, 0, 0, 0)),
            pl.BlockSpec((2, 2, levels, width), lambda i: (0, last_pair, 0, 0)),
        ]
        + whole(11),
        out_specs=whole(3),
        compiler_params=params,
        name="outer",
    )(
        above,
        below,
        partial_low,
        partial_high,
        air_here,
        air_here,
        wind_here,
        wind_here,
        packed,
        even_side,
        odd_side,
        near,
        physics,
        bottom,
        exchange_rate,
        sea_surface,
        weight_tile,
        remap_tiles,
        start,
    )

    if groups <= 4:
        turns = sorted(range(1, groups), key=lambda turn: abs(2 * turn - groups))
        gathered = [message] + [shift(message, "cpl", turn) for turn in turns]
    else:
        gathered = [message, lax.all_gather(message, "cpl")]

    air_next = pl.pallas_call(
        patch_kernel,
        out_shape=shape_of((rows, levels, width)),
        in_specs=[pl.BlockSpec(memory_space=pl.ANY)] * 2,
        out_specs=pl.BlockSpec(memory_space=pl.ANY),
        scratch_shapes=[pltpu.SemaphoreType.DMA((2,))],
        input_output_aliases={1: 0},
        compiler_params=params,
        name="patch",
    )(air_edges, air_inner)

    ocean_next, surface_temp = pl.pallas_call(
        make_last_kernel(len(gathered)),
        out_shape=(shape_of(ocean_shape), shape_of((rows, width))),
        in_specs=whole(len(gathered) + 7),
        out_specs=tuple(whole(2)),
        compiler_params=params,
        name="last",
    )(
        *gathered,
        base,
        response,
        total_weight,
        bottom_next,
        ocean_mask,
        weight_tile,
        remap_tiles,
    )
    return (air_next, ocean_next, surface_temp)


def solution(mesh):
    placed = (
        P("atm", None, "cpl"),
        P(None, "atm", None, "cpl"),
        P(),
        P("atm", "cpl"),
        P("atm", "cpl"),
        P("atm", "cpl"),
        P("cpl", "atm", None),
        P("cpl", "atm"),
        P("cpl", "atm"),
        P(),
        P(None, ("atm", "cpl")),
        P(),
    )
    return jax.shard_map(
        local,
        mesh=mesh,
        in_specs=placed,
        out_specs=(P("atm", None, "cpl"), P(None, ("atm", "cpl")), P("atm", "cpl")),
        check_vma=False,
    )
```

profile of v0, /device:TPU:0, one launch (start us, length us, event | category | flops | bytes accessed | tf_op | source)
XLA Modules:
  0.0 22.5 jit_solution(3215890607187543160)
XLA Ops:
  0.6 1.9 %pack.1 = (bf16[2,64,128]{2,1,0:T(8,128)(2,1)S(1)}, f32[24,64,128]{2,1,0:T(8,128)S(1)}, bf16[2,24,64,128]{3,2,1,0:T(8,128)(2,1)S(1)}, f32[64,64]{1,0:T(8,128)S(1...) custom-call(f32[24,64,128]{2,1,0:T(8,128)} %air.1, ...), custom_call_target="tpu_custom_call" | custom-call | tf_op jit(solution)/shard_map/pack/pallas_call | solution.py:542
  2.6 2.4 %collective-permute-start.1 = (bf16[2,64,128]{2,1,0:T(8,128)(2,1)S(1)}, bf16[2,64,128]{2,1,0:T(8,128)(2,1)S(1)}, u32[]{:S(2)}, u32[]{:S(2)}) collective-permute-start(bf16[2,64,128]{2,1,0:T(8,128)(2,1)S(1)} %get-tuple-element.35._.own), channel_id=1, source_target_pairs={{1,2},{3,0},{2,1},{0,3},{5,6},{7,4},{6,5},{4,7},{9,10},{11,8},{10,... | collective-permute-start | bytes 98312 | tf_op jit(solution)/shard_map/ppermute | solution.py:26
  5.0 0.7 %collective-permute-start = (bf16[2,64,128]{2,1,0:T(8,128)(2,1)S(1)}, bf16[2,64,128]{2,1,0:T(8,128)(2,1)S(1)}, u32[]{:S(2)}, u32[]{:S(2)}) collective-permute-start(bf16[2,64,128]{2,1,0:T(8,128)(2,1)S(1)} %get-tuple-element.35._.own), channel_id=1, source_target_pairs={{0,1},{1,0},{2,3},{3,2},{4,5},{5,4},{6,7},{7,6},{8,9},{9,8},{10,11... | collective-permute-start | bytes 98312 | tf_op jit(solution)/shard_map/ppermute | solution.py:27
  5.7 0.9 %start.1 = (f32[24,128]{1,0:T(8,128)S(1)}, f32[24,128]{1,0:T(8,128)S(1)}, f32[32,128]{1,0:T(8,128)S(1)}, f32[80,768]{1,0:T(8,128)S(1)}, f32[80,128]{1,0:T(8,128)S(1)}) custom-call(bf16[2,24,64,128]{3,2,1,0:T(8,128)(2,1)S(1)} %get-tuple-element.34.winds.wind.wind_low.wind_high, f32[24,128]{1,0:T(8,128)S(1)} %get-tuple-element.36.shortwave, ...), custom_call_target="tpu_custom_call" | custom-call | tf_op jit(solution)/shard_map/start/pallas_call | solution.py:560
  6.6 0.2 collective-permute-done.1.odd_side
  6.8 0.0 collective-permute-done.even_side
  6.8 0.2 edge.2
  7.0 2.5 %collective-permute-start.3 = (bf16[4,64,128]{2,1,0:T(8,128)(2,1)S(1)}, bf16[4,64,128]{2,1,0:T(8,128)(2,1)S(1)}, u32[]{:S(2)}, u32[]{:S(2)}) collective-permute-start(bf16[4,64,128]{2,1,0:T(8,128)(2,1)S(1)} %get-tuple-element.47), channel_id=1, source_target_pairs={{0,4},{4,8},{8,12},{12,16},{16,20},{20,24},{24,28},{28,0},{1,5},{5... | collective-permute-start | bytes 196616 | tf_op jit(solution)/shard_map/ppermute | solution.py:33
  9.5 0.2 edge.3
  9.6 3.1 %collective-permute-start.2 = (bf16[4,64,128]{2,1,0:T(8,128)(2,1)S(1)}, bf16[4,64,128]{2,1,0:T(8,128)(2,1)S(1)}, u32[]{:S(2)}, u32[]{:S(2)}) collective-permute-start(bf16[4,64,128]{2,1,0:T(8,128)(2,1)S(1)} %get-tuple-element.46), channel_id=1, source_target_pairs={{0,28},{4,0},{8,4},{12,8},{16,12},{20,16},{24,20},{28,24},{1,29},{... | collective-permute-start | bytes 196616 | tf_op jit(solution)/shard_map/ppermute | solution.py:33
  12.8 2.5 %inner.1 = (f32[24,64,128]{2,1,0:T(8,128)}, f32[4,64,128]{2,1,0:T(8,128)S(1)}, f32[24,128]{1,0:T(8,128)S(1)}) custom-call(f32[24,64,128]{2,1,0:T(8,128)S(1)} %get-tuple-element.33.air.air_low.air_high, bf16[2,24,64,128]{3,2,1,0:T(8,128)(2,1)S(1)} %get-tuple-element.34.winds.wind.wind_low.wind_high, f32[64,64]{1,0:T(8,128)S(1)} %get-tuple-element.49.physics, ...), custom_call_target="tpu_custom_call" | custom-call | tf_op jit(solution)/shard_map/inner/pallas_call | solution.py:616
  15.3 0.0 collective-permute-done.3.below_ref
  15.3 0.1 collective-permute-done.2.above_ref
  15.4 1.0 %outer.1 = (f32[4,64,128]{2,1,0:T(8,128)S(1)}, f32[24,128]{1,0:T(8,128)S(1)}, f32[32,128]{1,0:T(8,128)S(1)}) custom-call(bf16[4,64,128]{2,1,0:T(8,128)(2,1)S(1)} %collective-permute-done.2.above_ref, bf16[4,64,128]{2,1,0:T(8,128)(2,1)S(1)} %collective-permute-done.3.below_ref, f32[2,64,128]{2,1,0:T(8,128)S(1)} %get-tuple-element.48.partial_low, ...), custom_call_target="tpu_custom_call" | custom-call | tf_op jit(solution)/shard_map/outer/pallas_call | solution.py:634
  16.4 0.9 %collective-permute-start.6 = (f32[32,128]{1,0:T(8,128)S(1)}, f32[32,128]{1,0:T(8,128)S(1)}, u32[]{:S(2)}, u32[]{:S(2)}) collective-permute-start(f32[32,128]{1,0:T(8,128)S(1)} %get-tuple-element.56.refs_0_), channel_id=1, source_target_pairs={{0,3},{1,0},{2,1},{3,2},{4,7},{5,4},{6,5},{7,6},{8,11},{9,8},{10,9... | collective-permute-start | bytes 49160 | tf_op jit(solution)/shard_map/ppermute | solution.py:33
  17.3 0.0 collective-permute-start.5
  17.3 1.2 %collective-permute-start.4 = (f32[32,128]{1,0:T(8,128)S(1)}, f32[32,128]{1,0:T(8,128)S(1)}, u32[]{:S(2)}, u32[]{:S(2)}) collective-permute-start(f32[32,128]{1,0:T(8,128)S(1)} %get-tuple-element.56.refs_0_), channel_id=1, source_target_pairs={{0,2},{1,3},{2,0},{3,1},{4,6},{5,7},{6,4},{7,5},{8,10},{9,11},{10,... | collective-permute-start | bytes 49160 | tf_op jit(solution)/shard_map/ppermute | solution.py:33
  18.5 0.7 %patch.1 = f32[24,64,128]{2,1,0:T(8,128)} custom-call(f32[4,64,128]{2,1,0:T(8,128)S(1)} %get-tuple-element.54.edges, f32[24,64,128]{2,1,0:T(8,128)} %get-tuple-element.55._), custom_call_target="tpu_custom_call", output_to_operand_aliasing={{}: (1, {})} | custom-call | tf_op jit(solution)/shard_map/patch/pallas_call | solution.py:680
  19.2 0.0 collective-permute-done.6.refs_3_
  19.2 1.3 %collective-permute-done.5.refs_2_ = f32[32,128]{1,0:T(8,128)S(1)} collective-permute-done((f32[32,128]{1,0:T(8,128)S(1)}, f32[32,128]{1,0:T(8,128)S(1)}, u32[]{:S(2)}, u32[]{:S(2)}) %collective-permute-start.5) | collective-permute-done | bytes 16416 | tf_op jit(solution)/shard_map/ppermute | solution.py:33
  20.5 0.7 %collective-permute-done.4.refs_1_ = f32[32,128]{1,0:T(8,128)S(1)} collective-permute-done((f32[32,128]{1,0:T(8,128)S(1)}, f32[32,128]{1,0:T(8,128)S(1)}, u32[]{:S(2)}, u32[]{:S(2)}) %collective-permute-start.4) | collective-permute-done | bytes 16416 | tf_op jit(solution)/shard_map/ppermute | solution.py:33
  21.1 1.4 %last.1 = (f32[80,768]{1,0:T(8,128)}, f32[24,128]{1,0:T(8,128)}) custom-call(f32[32,128]{1,0:T(8,128)S(1)} %get-tuple-element.56.refs_0_, f32[32,128]{1,0:T(8,128)S(1)} %collective-permute-done.4.refs_1_, f32[32,128]{1,0:T(8,128)S(1)} %collective-permute-done.5.refs_2_, f32[32,128]{1,0:T(8,128)S(1)} %collective-permute-done.6.refs_3_, ...), custom_call_target="tpu_custom_call" | custom-call | tf_op jit(solution)/shard_map/last/pallas_call | solution.py:691
Async XLA Ops:
  2.6 4.2 %collective-permute-start.1 = (bf16[2,64,128]{2,1,0:T(8,128)(2,1)S(1)}, bf16[2,64,128]{2,1,0:T(8,128)(2,1)S(1)}, u32[]{:S(2)}, u32[]{:S(2)}) collective-permute-start(bf16[2,64,128]{2,1,0:T(8,128)(2,1)S(1)} %get-tuple-element.35._.own), channel_id=1, source_target_pairs={{1,2},{3,0},{2,1},{0,3},{5,6},{7,4},{6,5},{4,7},{9,10},{11,8},{10,... | collective-permute-start | bytes 98312 | tf_op jit(solution)/shard_map/ppermute | solution.py:26
  5.0 1.8 %collective-permute-start = (bf16[2,64,128]{2,1,0:T(8,128)(2,1)S(1)}, bf16[2,64,128]{2,1,0:T(8,128)(2,1)S(1)}, u32[]{:S(2)}, u32[]{:S(2)}) collective-permute-start(bf16[2,64,128]{2,1,0:T(8,128)(2,1)S(1)} %get-tuple-element.35._.own), channel_id=1, source_target_pairs={{0,1},{1,0},{2,3},{3,2},{4,5},{5,4},{6,7},{7,6},{8,9},{9,8},{10,11... | collective-permute-start | bytes 98312 | tf_op jit(solution)/shard_map/ppermute | solution.py:27
  7.0 8.3 %collective-permute-start.3 = (bf16[4,64,128]{2,1,0:T(8,128)(2,1)S(1)}, bf16[4,64,128]{2,1,0:T(8,128)(2,1)S(1)}, u32[]{:S(2)}, u32[]{:S(2)}) collective-permute-start(bf16[4,64,128]{2,1,0:T(8,128)(2,1)S(1)} %get-tuple-element.47), channel_id=1, source_target_pairs={{0,4},{4,8},{8,12},{12,16},{16,20},{20,24},{24,28},{28,0},{1,5},{5... | collective-permute-start | bytes 196616 | tf_op jit(solution)/shard_map/ppermute | solution.py:33
  9.6 5.7 %collective-permute-start.2 = (bf16[4,64,128]{2,1,0:T(8,128)(2,1)S(1)}, bf16[4,64,128]{2,1,0:T(8,128)(2,1)S(1)}, u32[]{:S(2)}, u32[]{:S(2)}) collective-permute-start(bf16[4,64,128]{2,1,0:T(8,128)(2,1)S(1)} %get-tuple-element.46), channel_id=1, source_target_pairs={{0,28},{4,0},{8,4},{12,8},{16,12},{20,16},{24,20},{28,24},{1,29},{... | collective-permute-start | bytes 196616 | tf_op jit(solution)/shard_map/ppermute | solution.py:33
  16.4 2.8 %collective-permute-start.6 = (f32[32,128]{1,0:T(8,128)S(1)}, f32[32,128]{1,0:T(8,128)S(1)}, u32[]{:S(2)}, u32[]{:S(2)}) collective-permute-start(f32[32,128]{1,0:T(8,128)S(1)} %get-tuple-element.56.refs_0_), channel_id=1, source_target_pairs={{0,3},{1,0},{2,1},{3,2},{4,7},{5,4},{6,5},{7,6},{8,11},{9,8},{10,9... | collective-permute-start | bytes 49160 | tf_op jit(solution)/shard_map/ppermute | solution.py:33
  17.3 3.2 %collective-permute-start.5 = (f32[32,128]{1,0:T(8,128)S(1)}, f32[32,128]{1,0:T(8,128)S(1)}, u32[]{:S(2)}, u32[]{:S(2)}) collective-permute-start(f32[32,128]{1,0:T(8,128)S(1)} %get-tuple-element.56.refs_0_), channel_id=1, source_target_pairs={{0,1},{1,2},{2,3},{3,0},{4,5},{5,6},{6,7},{7,4},{8,9},{9,10},{10,1... | collective-permute-start | bytes 49160 | tf_op jit(solution)/shard_map/ppermute | solution.py:33
  17.3 3.8 %collective-permute-start.4 = (f32[32,128]{1,0:T(8,128)S(1)}, f32[32,128]{1,0:T(8,128)S(1)}, u32[]{:S(2)}, u32[]{:S(2)}) collective-permute-start(f32[32,128]{1,0:T(8,128)S(1)} %get-tuple-element.56.refs_0_), channel_id=1, source_target_pairs={{0,2},{1,3},{2,0},{3,1},{4,6},{5,7},{6,4},{7,5},{8,10},{9,11},{10,... | collective-permute-start | bytes 49160 | tf_op jit(solution)/shard_map/ppermute | solution.py:33
where the time goes:
time: 22.7 us; the launch traced here: 22.5 us
  starting transfers between devices  10.9 us (48%)
  Pallas kernels  8.76 us (39%)
  waiting for transfers between devices  2.17 us (10%)
  between operations  0.7 us (3%)
    ppermute x5, starting transfers between devices, shift(): lax.ppermute(block, axis, [(i, (i + turn) % count) for i in range(count)])  7.76 us
    pallas_call x1, Pallas kernels, local(): pl.pallas_call(inner_kernel, out_shape=(shape_of((rows, levels, width)),...  2.53 us
    ppermute x1, starting transfers between devices, exchange(): odd_side = lax.ppermute(block, axis, pair_odd(count))  2.44 us
    ppermute x5, waiting for transfers between devices, shift(): lax.ppermute(block, axis, [(i, (i + turn) % count) for i in range(count)])  1.98 us
    pallas_call x1, Pallas kernels, local(): pl.pallas_call(pack_kernel, out_shape=(pltpu.VMEM((2, levels, width), bf1...  1.93 us
    pallas_call x1, Pallas kernels, local(): pl.pallas_call(make_last_kernel(len(gathered)), out_shape=(shape_of(ocean...  1.35 us
    pallas_call x1, Pallas kernels, local(): pl.pallas_call(make_outer_kernel(rows), grid=(1,), out_shape=(shape_of((4...  1.03 us
    pallas_call x1, Pallas kernels, local(): pl.pallas_call(start_kernel, grid=(1,), out_shape=(shape_of((rows, width)...  0.92 us
  transfers between devices with their start and end apart: 7, of which 4 were waited for; matrix products, arithmetic and copies ran while one was open for 0% of the time, Pallas kernels for 19%

commit v1 on v0

--- a/solution.py
+++ b/solution.py
@@ -21,10 +21,10 @@
     return up + [(target, source) for source, target in up]
 
 
-def exchange(block, axis):
+def exchange(to_even, to_odd, axis):
     count = lax.axis_size(axis)
-    odd_side = lax.ppermute(block, axis, pair_odd(count))
-    even_side = lax.ppermute(block, axis, pair_even(count))
+    odd_side = lax.ppermute(to_odd, axis, pair_odd(count))
+    even_side = lax.ppermute(to_even, axis, pair_even(count))
     return even_side, odd_side
 
 
@@ -73,8 +73,8 @@
 
 
 def pack_kernel(air, wind, *refs):
-    others = (len(refs) - 5) // 2
-    packed, air_here, wind_here = refs[others : others + 3]
+    others = (len(refs) - 7) // 2
+    packed, to_even, to_odd, air_here, wind_here = refs[others : others + 5]
     sems, other_sems = refs[-2:]
     rows, levels, width = air.shape
     lane = iota((levels, width), 1)
@@ -95,24 +95,29 @@
             copy.start()
     later = [
         pltpu.make_async_copy(source, target, other_sems.at[at])
-        for at, (source, target) in enumerate(zip(refs[:others], refs[others + 3 : -2]))
+        for at, (source, target) in enumerate(zip(refs[:others], refs[others + 5 : -2]))
     ]
     for copy in later:
         copy.start()
-    cells = jnp.zeros((levels, width), f32)
-    first = jnp.zeros((levels, width), f32)
-    second = jnp.zeros((levels, width), f32)
+    cells = jnp.zeros((levels, width), bf16)
+    first = jnp.zeros((levels, width), bf16)
+    second = jnp.zeros((levels, width), bf16)
     for x in range(rows):
         if x % size == 0:
             for copy in copies[x // size]:
                 copy.wait()
         here = place == x
-        cells = pick(here, roll(air_here[x], 4 * x + 2), cells)
-        first = pick(here, roll(wind_here[0, x].astype(f32), 4 * x + 2), first)
-        second = pick(here, roll(wind_here[1, x].astype(f32), 4 * x + 2), second)
+        cells = pick(here, roll(air_here[x].astype(bf16), 4 * x + 2), cells)
+        first = pick(here, roll(wind_here[0, x], 4 * x + 2), first)
+        second = pick(here, roll(wind_here[1, x], 4 * x + 2), second)
+    cells, first, second = (value.astype(f32) for value in (cells, first, second))
     winds = pick((kind == 1) | (kind == 2), first, roll(second, 2))
-    packed[0] = cells.astype(bf16)
-    packed[1] = winds.astype(bf16)
+    to_high = pick(kind < 2, cells, pick(kind == 2, roll(winds, 1), winds))
+    to_low = pick(kind >= 2, cells, pick(kind == 0, roll(winds, -2), roll(winds, -3)))
+    upper = lax.axis_index("cpl") % 2 == 0
+    packed[...] = cells
+    to_even[...] = pick(upper, to_high, to_low).astype(bf16)
+    to_odd[...] = pick(upper, to_low, to_high).astype(bf16)
     for copy in later:
         copy.wait()
 
@@ -125,8 +130,8 @@
 
 
 def outer_cells(low, high):
-    kind = iota(low.shape[1:], 1) % 4
-    return pick(kind < 2, low[0], high[0])
+    kind = iota(low.shape, 1) % 4
+    return pick(kind < 2, low, high)
 
 
 def swap_cells(cells):
@@ -156,9 +161,22 @@
     kind = iota(outer.shape, 1) % 4
     south = roll(pick(kind == 0, outer, own), 1)
     north = roll(pick(kind == 3, outer, own), -1)
-    first = pick(kind == 1, low[1], high[1])
-    second = roll(pick(kind == 3, low[1], high[1]), -2)
+    first = pick(kind == 1, roll(low, -1), roll(high, 2))
+    second = pick(kind == 1, roll(low, -2), roll(high, 1))
     return advance_row(outer, west, east, south, north, rates(first, second))
+
+
+def pack_corners(outer, x):
+    levels, width = outer.shape
+    place = iota((8, width), 1) // 4
+    held = jnp.zeros((8, width), f32)
+    for at in range(levels // 8):
+        held = pick(place == at, roll(outer[8 * at : 8 * at + 8], 4 * (at - x)), held)
+    return jnp.concatenate([held, jnp.zeros_like(held)], axis=0)
+
+
+def unpack_corners(held, levels, x):
+    return jnp.concatenate([roll(held[0:8], 4 * (x - at)) for at in range(levels // 8)], axis=0)
 
 
 def make_edge_kernel(rows, upper):
@@ -166,6 +184,7 @@
         low, high = cpl_sides(even_side, odd_side)
         outer = outer_cells(low, high)
         center, inner = (air[1], air[0]) if upper else (air[0], air[1])
+        levels = center.shape[0]
         cw, ce, cs, cn = rates(wind[0, 0].astype(f32), wind[1, 0].astype(f32))
         inside, outside = (cw, ce) if upper else (ce, cw)
         south, north = sideways(center, swap_cells(outer), rows - 1 if upper else 0)
@@ -176,22 +195,23 @@
         )
         partial[0] = known
         partial[1] = outside
-        for at, value in enumerate((center, known, outside, outer)):
-            message[at] = value.astype(bf16)
+        for at, value in enumerate((center, known, outside)):
+            message[at * levels : (at + 1) * levels] = value.astype(bf16)
+        message[3 * levels :] = pack_corners(outer, rows - 1 if upper else 0).astype(bf16)
 
     return edge_kernel
 
 
 def inner_kernel(
-    air, wind, physics, own, even_side, odd_side, air_next, near, bottom, field, ready, sems
+    air, wind, stack_ref, own, even_side, odd_side, ready, near, bottom, field
 ):
     rows, levels, width = air.shape
     low, high = cpl_sides(even_side, odd_side)
     outer = outer_cells(low, high)
-    stack = physics_stack(physics[...])
+    stack = stack_ref[...]
     swapped = swap_cells(outer)
     after = advance_outer(
-        own[0].astype(f32), low, high, outer, roll(outer, 4), roll(outer, -4)
+        own[...], low, high, outer, roll(outer, 4), roll(outer, -4)
     )
     swapped_after = swap_cells(column(stack, after))
 
@@ -215,18 +235,12 @@
     near[2] = field[rows - 3]
     near[3] = field[rows - 2]
     bottom[...] = jnp.zeros_like(bottom)
-    copies = []
     for x in range(2, rows - 2, 2):
         both = pair(field, swapped_after, x)
         ready[x] = both[:, :width]
         ready[x + 1] = both[:, width:]
         bottom[x : x + 1] = both[0:1, :width]
         bottom[x + 1 : x + 2] = both[0:1, width:]
-        span = pl.ds(x, 2)
-        copies.append(pltpu.make_async_copy(ready.at[span], air_next.at[span], sems.at[x // 2 - 1]))
-        copies[-1].start()
-    for copy in copies:
-        copy.wait()
 
 
 def as_column(row):
@@ -247,26 +261,42 @@
     return value
 
 
-def chosen_shares(fluxes, weights, bank, ocean_width):
+def chosen_shares(fluxes, halves, bank, ocean_width):
     rows, width = fluxes.shape
-    every = lax.dot_general(
-        fluxes, weights, (((1,), (1,)), ((), ())), precision=highest, preferred_element_type=f32
+    high, low = split(fluxes)
+    every = jnp.dot(
+        jnp.concatenate([high, low, high], axis=1), halves, preferred_element_type=f32
     )
     total = jnp.zeros((rows, width), f32)
-    for at in range(0, weights.shape[0], width):
+    for at in range(0, halves.shape[1], width):
         block = (iota((rows, width), 1) + at) // ocean_width
         total = total + jnp.where(block == bank, every[:, at : at + width], 0.0)
     return fold(total, ocean_width)
 
 
 def start_kernel(
-    winds, shortwave, mask, route, tile, bank, weights, ocean, mixing, _,
-    exchange_rate, total_weight, message, base, response,
+    winds, shortwave, mask, route, tile, bank, physics, weights_far, ocean_far, mixing_far, _,
+    exchange_rate, message, forward, backward, stack, weights, ocean, mixing, sems,
 ):
+    copies = [
+        pltpu.make_async_copy(source, target, sems.at[at])
+        for at, (source, target) in enumerate(
+            ((weights_far, weights), (ocean_far, ocean), (mixing_far, mixing))
+        )
+    ]
+    for copy in copies:
+        copy.start()
+    stack[...] = physics_stack(physics[...])
+    for copy in copies:
+        copy.wait()
     rows, width = shortwave.shape
-    depth = ocean.shape[0]
     banks, ocean_width, _ = weights.shape
     flat = weights[...].reshape(banks * ocean_width, width)
+    high, low = split(flat)
+    backward[...] = jnp.concatenate([high, high, low], axis=0)
+    turned = flat.T
+    high, low = split(turned)
+    forward[...] = jnp.concatenate([high, high, low], axis=0)
     frac = mask[...].astype(f32)
     bank_at = as_column(bank[...].astype(f32)).astype(jnp.int32)
     for x in range(rows):
@@ -274,25 +304,11 @@
         second = winds[1, x].astype(f32)[0:1]
         exchange_rate[x : x + 1] = first * first + second * second
     exchange_rate[...] = frac * (0.5 + 2.0 * jnp.sqrt(exchange_rate[...] + 0.01))
-    solar = chosen_shares(frac * shortwave[...], flat, bank_at, ocean_width)
+    solar = chosen_shares(frac * shortwave[...], forward[...], bank_at, ocean_width)
     lane = iota((rows, width), 1)
-    total = jnp.zeros((rows, width), f32)
-    for at in range(0, banks * ocean_width, width):
-        hot = ((lane + at) // ocean_width == bank_at).astype(f32)
-        total = total + jnp.dot(hot, flat[at : at + width], precision=highest, preferred_element_type=f32)
-    total_weight[...] = total
-
-    held = ocean[...]
-    mixed = mixing[...]
-    settled = 0.5 * held + jnp.dot(mixed, held, precision=highest, preferred_element_type=f32)
-    base[...] = settled
-    level = iota((depth, width), 0)
-    profile = jnp.exp(level.astype(f32) / -8.0)
-    profile = profile / jnp.sum(profile, axis=0, keepdims=True)
-    part = iota((depth, width), 1)
-    unit = jnp.where(part == 0, (level == 0).astype(f32), jnp.where(part == 1, profile, 0.0))
-    response[...] = 0.5 * unit + jnp.dot(mixed, unit, precision=highest, preferred_element_type=f32)
-
+    settled = 0.5 * ocean[0:8] + jnp.dot(
+        mixing[0:8], ocean[...], precision=highest, preferred_element_type=f32
+    )
     group = lax.axis_index("cpl")
     surface = jnp.zeros((rows, width), f32)
     for at in range(0, rows * ocean_width, width):
@@ -321,24 +337,27 @@
 def make_outer_kernel(rows):
     def outer_kernel(
         above_ref, below_ref, partial_low, partial_high, air_low, air_high, wind_low, wind_high, own, even_side, odd_side,
-        near, physics, bottom, rate, sea, bank, weights, start,
+        near, stack_ref, bottom, rate, sea, bank, forward, start,
         air_edges, bottom_next, message,
     ):
         width = sea.shape[1]
-        banks, ocean_width, _ = weights.shape
-        above = above_ref[...].astype(f32)
-        below = below_ref[...].astype(f32)
+        ocean_width = start.shape[0]
+        levels = air_low.shape[1]
+        above = [above_ref[at * levels : (at + 1) * levels].astype(f32) for at in range(3)]
+        below = [below_ref[at * levels : (at + 1) * levels].astype(f32) for at in range(3)]
+        above.append(unpack_corners(above_ref[3 * levels :].astype(f32), levels, rows - 1))
+        below.append(unpack_corners(below_ref[3 * levels :].astype(f32), levels, 0))
         low, high = cpl_sides(even_side, odd_side)
         outer = outer_cells(low, high)
-        stack = physics_stack(physics[...])
+        stack = stack_ref[...]
         place = iota(outer.shape, 1) // 4
         after = advance_outer(
-            own[0].astype(f32),
+            own[...],
             low,
             high,
             outer,
-            pick(place == 0, roll(below[3], -4 * (rows - 1)), roll(outer, 4)),
-            pick(place == rows - 1, roll(above[3], 4 * (rows - 1)), roll(outer, -4)),
+            pick(place == 0, below[3], roll(outer, 4)),
+            pick(place == rows - 1, above[3], roll(outer, -4)),
         )
         moved = jnp.concatenate(
             [
@@ -371,9 +390,8 @@
             air_edges[at] = row
             bottom_next[x : x + 1] = row[0:1]
         heat = rate[...] * (bottom_next[...] - sea[...])
-        flat = weights[...].reshape(banks * ocean_width, width)
         bank_at = as_column(bank[...].astype(f32)).astype(jnp.int32)
-        shares = chosen_shares(heat, flat, bank_at, ocean_width)
+        shares = chosen_shares(heat, forward[...], bank_at, ocean_width)
         message[...] = start[...]
         message[0:rows, :] = jnp.where(
             iota((rows, width), 1) < ocean_width, shares, start[0:rows, :]
@@ -382,21 +400,43 @@
     return outer_kernel
 
 
-def patch_kernel(edges, _, out, sems):
+def settle_kernel(
+    edges, inner, bank, weights, ocean, mixing, out, base, response, total_weight, sems
+):
     rows = out.shape[0]
+    middle = pl.ds(2, rows - 4)
     copies = [
+        pltpu.make_async_copy(inner.at[middle], out.at[middle], sems.at[2]),
         pltpu.make_async_copy(edges.at[pl.ds(0, 2)], out.at[pl.ds(0, 2)], sems.at[0]),
         pltpu.make_async_copy(edges.at[pl.ds(2, 2)], out.at[pl.ds(rows - 2, 2)], sems.at[1]),
     ]
     for copy in copies:
         copy.start()
+    width = total_weight.shape[1]
+    depth = ocean.shape[0]
+    banks, ocean_width, _ = weights.shape
+    sums = jnp.concatenate(
+        [jnp.sum(weights[at], axis=0, keepdims=True) for at in range(banks)], axis=0
+    )
+    bank_at = as_column(bank[...].astype(f32)).astype(jnp.int32)
+    hot = (iota((rows, banks), 1) == bank_at).astype(f32)
+    total_weight[...] = jnp.dot(hot, sums, precision=highest, preferred_element_type=f32)
+    mixed = mixing[...]
+    held = ocean[...]
+    base[...] = 0.5 * held + jnp.dot(mixed, held, precision=highest, preferred_element_type=f32)
+    level = iota((depth, width), 0)
+    profile = jnp.exp(level.astype(f32) / -8.0)
+    profile = profile / jnp.sum(profile, axis=0, keepdims=True)
+    part = iota((depth, width), 1)
+    unit = jnp.where(part == 0, (level == 0).astype(f32), jnp.where(part == 1, profile, 0.0))
+    response[...] = 0.5 * unit + jnp.dot(mixed, unit, precision=highest, preferred_element_type=f32)
     for copy in copies:
         copy.wait()
 
 
 def make_last_kernel(count):
     def last_kernel(*refs):
-        messages, (base, response, total_weight, bottom, mask, bank, weights, ocean_next, surface) = (
+        messages, (base, response, total_weight, bottom, mask, bank, backward, ocean_next, surface, ocean_here, surface_here, sems) = (
             refs[:count],
             refs[count:],
         )
@@ -406,9 +446,9 @@
         else:
             blocks = [ref[...] for ref in messages]
         rows, width = bottom.shape
-        banks, ocean_width, _ = weights.shape
         slots = own.shape[0]
-        depth = base.shape[0]
+        ocean_width = slots
+        cells = backward.shape[0] // 3
         own_part = own[0:rows]
         wanted = jnp.concatenate(
             [
@@ -424,7 +464,7 @@
         values = []
         for block in blocks:
             label = block[rows : rows + 1, 0 : 2 * ocean_width]
-            hot.append((wanted == label).astype(f32))
+            hot.append((wanted == label).astype(f32).astype(bf16))
             raised = top * roll(block, 2 * ocean_width) + sun * roll(block, ocean_width)
             values.append(
                 jnp.where(
@@ -434,10 +474,10 @@
             values.append(
                 jnp.where((lane >= 2 * ocean_width) & (lane < 3 * ocean_width), block, 0.0)
             )
+        high, low = split(jnp.concatenate(values, axis=0))
         got = jnp.dot(
-            jnp.concatenate(hot, axis=1),
-            jnp.concatenate(values, axis=0),
-            precision=highest,
+            jnp.concatenate(hot + hot, axis=1),
+            jnp.concatenate([high, low], axis=0),
             preferred_element_type=f32,
         )
         near = iota((rows, width), 1)
@@ -447,6 +487,19 @@
             ),
             ocean_width,
         )
+        bank_at = as_column(bank[...].astype(f32)).astype(jnp.int32)
+        high, low = split(
+            jnp.concatenate(
+                [
+                    jnp.where((near + at) // ocean_width == bank_at, seen, 0.0)
+                    for at in range(0, cells, width)
+                ],
+                axis=1,
+            )
+        )
+        weighted = jnp.dot(
+            jnp.concatenate([high, low, high], axis=1), backward[...], preferred_element_type=f32
+        )
         forcing = got[rows : 2 * rows]
         heat = fold(jnp.where(near < ocean_width, forcing, 0.0), ocean_width)
         solar = fold(
@@ -458,21 +511,17 @@
             mine = (near + at) // ocean_width == iota((rows, width), 0)
             heat_row = jnp.sum(jnp.where(mine, heat, 0.0), axis=0, keepdims=True)
             solar_row = jnp.sum(jnp.where(mine, solar, 0.0), axis=0, keepdims=True)
-            ocean_next[:, at : at + width] = base[:, at : at + width] + (
+            ocean_here[:, at : at + width] = base[:, at : at + width] + (
                 first * heat_row + second * solar_row
             )
-        flat = weights[...].reshape(banks * ocean_width, width)
-        bank_at = as_column(bank[...].astype(f32)).astype(jnp.int32)
-        spread = jnp.concatenate(
-            [
-                jnp.where((near + at) // ocean_width == bank_at, seen, 0.0)
-                for at in range(0, banks * ocean_width, width)
-            ],
-            axis=1,
-        )
-        weighted = jnp.dot(spread, flat, precision=highest, preferred_element_type=f32)
+        ocean_out = pltpu.make_async_copy(ocean_here, ocean_next, sems.at[0])
+        ocean_out.start()
         frac = mask[...].astype(f32)
-        surface[...] = frac * (weighted / total_weight[...]) + (1.0 - frac) * bottom[...]
+        surface_here[...] = frac * (weighted / total_weight[...]) + (1.0 - frac) * bottom[...]
+        surface_out = pltpu.make_async_copy(surface_here, surface, sems.at[1])
+        surface_out.start()
+        ocean_out.wait()
+        surface_out.wait()
 
     return last_kernel
 
@@ -520,12 +569,11 @@
         owner_route.reshape(1, rows),
         ocean_tile,
         weight_tile,
-        remap_tiles,
-        ocean_temp,
-        mixing,
     )
     (
         packed,
+        to_even,
+        to_odd,
         air_here,
         wind_here,
         physics,
@@ -535,18 +583,19 @@
         owner_route,
         ocean_tile,
         weight_tile,
-        remap_tiles,
-        ocean_temp,
-        mixing,
     ) = (
         pl.pallas_call(
             pack_kernel,
-            out_shape=(pltpu.VMEM((2, levels, width), bf16),)
+            out_shape=(
+                pltpu.VMEM((levels, width), f32),
+                pltpu.VMEM((levels, width), bf16),
+                pltpu.VMEM((levels, width), bf16),
+            )
             + tuple(
                 pltpu.VMEM(value.shape, value.dtype) for value in (air_temp, wind_field) + others
             ),
             in_specs=[pl.BlockSpec(memory_space=pltpu.HBM)] * (2 + len(others)),
-            out_specs=tuple(whole(3 + len(others))),
+            out_specs=tuple(whole(5 + len(others))),
             scratch_shapes=[
                 pltpu.SemaphoreType.DMA((2, 2)),
                 pltpu.SemaphoreType.DMA((len(others),)),
@@ -555,22 +604,27 @@
             name="pack",
         )(*(in_hbm(value) for value in (air_temp, wind_field) + others))
     )
-    even_side, odd_side = exchange(packed, "cpl")
-
-    exchange_rate, total_weight, start, base, response = pl.pallas_call(
+    even_side, odd_side = exchange(to_even, to_odd, "cpl")
+
+    exchange_rate, start, forward, backward, stack, remap_tiles, ocean_temp, mixing = pl.pallas_call(
         start_kernel,
         grid=(1,),
         out_shape=(
             shape_of((rows, width)),
-            shape_of((rows, width)),
             shape_of((slots, width)),
-            shape_of(ocean_shape),
-            shape_of((ocean_shape[0], width)),
+            shape_of((3 * width, remap_tiles.shape[0] * ocean_width), bf16),
+            shape_of((3 * remap_tiles.shape[0] * ocean_width, width), bf16),
+            shape_of((levels, 3 * levels), bf16),
+            pltpu.VMEM(remap_tiles.shape, f32),
+            pltpu.VMEM(ocean_shape, f32),
+            pltpu.VMEM(mixing.shape, f32),
         ),
         in_specs=[pl.BlockSpec((2, rows, 16, width), lambda i: (0, 0, 0, 0))]
-        + whole(8)
+        + whole(6)
+        + [pl.BlockSpec(memory_space=pltpu.HBM)] * 3
         + [pl.BlockSpec(memory_space=pl.ANY)],
-        out_specs=whole(5),
+        out_specs=whole(8),
+        scratch_shapes=[pltpu.SemaphoreType.DMA((3,))],
         compiler_params=params,
         name="start",
     )(
@@ -580,9 +634,10 @@
         owner_route,
         ocean_tile,
         weight_tile,
-        remap_tiles,
-        ocean_temp,
-        mixing,
+        physics,
+        in_hbm(remap_tiles),
+        in_hbm(ocean_temp),
+        in_hbm(mixing),
         packed,
     )
 
@@ -596,7 +651,7 @@
         return pl.pallas_call(
             make_edge_kernel(rows, upper),
             grid=(1,),
-            out_shape=(shape_of((4, levels, width), bf16), shape_of((2, levels, width))),
+            out_shape=(shape_of((3 * levels + 16, width), bf16), shape_of((2, levels, width))),
             in_specs=[
                 air_specs[upper],
                 pl.BlockSpec((2, 1, levels, width), lambda i: (0, (rows - 1) * upper, 0, 0)),
@@ -616,20 +671,16 @@
     air_inner, near, bottom = pl.pallas_call(
         inner_kernel,
         out_shape=(
-            shape_of((rows, levels, width)),
+            pltpu.VMEM((rows, levels, width), f32),
             shape_of((4, levels, width)),
             shape_of((rows, width)),
         ),
         in_specs=whole(6),
-        out_specs=tuple([pl.BlockSpec(memory_space=pltpu.HBM)] + whole(2)),
-        scratch_shapes=[
-            pltpu.VMEM((rows, levels, width), f32),
-            pltpu.VMEM((rows, levels, width), f32),
-            pltpu.SemaphoreType.DMA((rows // 2 - 2,)),
-        ],
+        out_specs=tuple(whole(3)),
+        scratch_shapes=[pltpu.VMEM((rows, levels, width), f32)],
         compiler_params=params,
         name="inner",
-    )(air_here, wind_here, physics, packed, even_side, odd_side)
+    )(air_here, wind_here, stack, packed, even_side, odd_side)
 
     air_edges, bottom_next, message = pl.pallas_call(
         make_outer_kernel(rows),
@@ -662,12 +713,12 @@
         even_side,
         odd_side,
         near,
-        physics,
+        stack,
         bottom,
         exchange_rate,
         sea_surface,
         weight_tile,
-        remap_tiles,
+        forward,
         start,
     )
 
@@ -677,22 +728,31 @@
     else:
         gathered = [message, lax.all_gather(message, "cpl")]
 
-    air_next = pl.pallas_call(
-        patch_kernel,
-        out_shape=shape_of((rows, levels, width)),
-        in_specs=[pl.BlockSpec(memory_space=pl.ANY)] * 2,
-        out_specs=pl.BlockSpec(memory_space=pl.ANY),
-        scratch_shapes=[pltpu.SemaphoreType.DMA((2,))],
-        input_output_aliases={1: 0},
+    air_next, base, response, total_weight = pl.pallas_call(
+        settle_kernel,
+        out_shape=(
+            shape_of((rows, levels, width)),
+            shape_of(ocean_shape),
+            shape_of((ocean_shape[0], width)),
+            shape_of((rows, width)),
+        ),
+        in_specs=whole(6),
+        out_specs=tuple([pl.BlockSpec(memory_space=pltpu.HBM)] + whole(3)),
+        scratch_shapes=[pltpu.SemaphoreType.DMA((3,))],
         compiler_params=params,
-        name="patch",
-    )(air_edges, air_inner)
+        name="settle",
+    )(air_edges, air_inner, weight_tile, remap_tiles, ocean_temp, mixing)
 
     ocean_next, surface_temp = pl.pallas_call(
         make_last_kernel(len(gathered)),
         out_shape=(shape_of(ocean_shape), shape_of((rows, width))),
         in_specs=whole(len(gathered) + 7),
-        out_specs=tuple(whole(2)),
+        out_specs=(pl.BlockSpec(memory_space=pltpu.HBM),) * 2,
+        scratch_shapes=[
+            pltpu.VMEM(ocean_shape, f32),
+            pltpu.VMEM((rows, width), f32),
+            pltpu.SemaphoreType.DMA((2,)),
+        ],
         compiler_params=params,
         name="last",
     )(
@@ -703,7 +763,7 @@
         bottom_next,
         ocean_mask,
         weight_tile,
-        remap_tiles,
+        backward,
     )
     return (air_next, ocean_next, surface_temp)
 

time: 22.7 us -> 21.7 us (0.956)
  starting transfers between devices: 10.9 us -> 9.98 us
    ppermute x5, starting transfers between devices: 7.76 us -> 6.85 us  [shift(): lax.ppermute(block, axis, [(i, (i + turn) % count) for i in range(count)])]
    pallas_call x1, Pallas kernels: 0.92 us -> 1.57 us  [local(): pl.pallas_call(start_kernel, grid=(1,), out_shape=(shape_of((rows, width)...]
    pallas_call x3, Pallas kernels: 5.13 us -> 4.58 us  [the longest x1 1.88 us: local(): pl.pallas_call(pack_kernel, out_shape=(pltpu.VMEM((levels, width), f32),...]
  transfers between devices with their start and end apart: 7 -> 7, of which waited for: 4 -> 3; matrix products, arithmetic and copies ran while one was open for 0% -> 0% of each run, Pallas kernels for 19% -> 21%
where the time goes in v1:
time: 21.7 us; the launch traced here: 21.5 us
  starting transfers between devices  9.98 us (46%)
  Pallas kernels  8.78 us (40%)
  waiting for transfers between devices  2.03 us (9%)
  between operations  0.71 us (3%)
    ppermute x5, starting transfers between devices, shift(): lax.ppermute(block, axis, [(i, (i + turn) % count) for i in range(count)])  6.85 us
    ppermute x1, starting transfers between devices, exchange(): odd_side = lax.ppermute(to_odd, axis, pair_odd(count))  2.61 us
    ppermute x5, waiting for transfers between devices, shift(): lax.ppermute(block, axis, [(i, (i + turn) % count) for i in range(count)])  2.03 us
    pallas_call x1, Pallas kernels, local(): pl.pallas_call(pack_kernel, out_shape=(pltpu.VMEM((levels, width), f32),...  1.88 us
    pallas_call x1, Pallas kernels, local(): pl.pallas_call(inner_kernel, out_shape=(pltpu.VMEM((rows, levels, width),...  1.8 us
    pallas_call x1, Pallas kernels, local(): pl.pallas_call(start_kernel, grid=(1,), out_shape=(shape_of((rows, width)...  1.57 us
    pallas_call x1, Pallas kernels, local(): pl.pallas_call(make_last_kernel(len(gathered)), out_shape=(shape_of(ocean...  1.38 us
    pallas_call x1, Pallas kernels, local(): pl.pallas_call(make_outer_kernel(rows), grid=(1,), out_shape=(shape_of((4...  0.92 us
  transfers between devices with their start and end apart: 7, of which 3 were waited for; matrix products, arithmetic and copies ran while one was open for 0% of the time, Pallas kernels for 21%

profile of v1, /device:TPU:0, one launch (start us, length us, event | category | flops | bytes accessed | tf_op | source)
XLA Modules:
  0.0 21.5 jit_solution(2799624011093223681)
XLA Ops:
  0.6 1.9 %pack.1 = (f32[64,128]{1,0:T(8,128)S(1)}, bf16[64,128]{1,0:T(8,128)(2,1)S(1)}, bf16[64,128]{1,0:T(8,128)(2,1)S(1)}, f32[24,64,128]{2,1,0:T(8,128)S(1)}, bf16[2,2...) custom-call(f32[24,64,128]{2,1,0:T(8,128)} %air.1, ...), custom_call_target="tpu_custom_call" | custom-call | tf_op jit(solution)/shard_map/pack/pallas_call | solution.py:587
  2.5 0.5 %collective-permute-start = (bf16[64,128]{1,0:T(8,128)(2,1)S(1)}, bf16[64,128]{1,0:T(8,128)(2,1)S(1)}, u32[]{:S(2)}, u32[]{:S(2)}) collective-permute-start(bf16[64,128]{1,0:T(8,128)(2,1)S(1)} %get-tuple-element.41), channel_id=1, source_target_pairs={{0,1},{1,0},{2,3},{3,2},{4,5},{5,4},{6,7},{7,6},{8,9},{9,8},{10,11... | collective-permute-start | bytes 49160 | tf_op jit(solution)/shard_map/ppermute | solution.py:27
  3.0 2.6 %collective-permute-start.1 = (bf16[64,128]{1,0:T(8,128)(2,1)S(1)}, bf16[64,128]{1,0:T(8,128)(2,1)S(1)}, u32[]{:S(2)}, u32[]{:S(2)}) collective-permute-start(bf16[64,128]{1,0:T(8,128)(2,1)S(1)} %get-tuple-element.42), channel_id=1, source_target_pairs={{1,2},{3,0},{2,1},{0,3},{5,6},{7,4},{6,5},{4,7},{9,10},{11,8},{10,... | collective-permute-start | bytes 49160 | tf_op jit(solution)/shard_map/ppermute | solution.py:26
  5.7 1.6 %start.1 = (f32[24,128]{1,0:T(8,128)S(1)}, f32[32,128]{1,0:T(8,128)S(1)}, bf16[384,512]{1,0:T(8,128)(2,1)S(1)}, bf16[1536,128]{1,0:T(8,128)(2,1)S(1)}, bf16[64,1...) custom-call(bf16[2,24,64,128]{3,2,1,0:T(8,128)(2,1)S(1)} %get-tuple-element.40.wi, ...), custom_call_target="tpu_custom_call" | custom-call | tf_op jit(solution)/shard_map/start/pallas_call | solution.py:609
  7.2 0.0 collective-permute-done.even_side
  7.2 0.0 collective-permute-done.1.odd_side
  7.2 0.2 edge.2
  7.4 1.6 %collective-permute-start.3 = (bf16[208,128]{1,0:T(8,128)(2,1)S(1)}, bf16[208,128]{1,0:T(8,128)(2,1)S(1)}, u32[]{:S(2)}, u32[]{:S(2)}) collective-permute-start(bf16[208,128]{1,0:T(8,128)(2,1)S(1)} %get-tuple-element.53), channel_id=1, source_target_pairs={{0,4},{4,8},{8,12},{12,16},{16,20},{20,24},{24,28},{28,0},{1,5},{5... | collective-permute-start | bytes 159752 | tf_op jit(solution)/shard_map/ppermute | solution.py:33
  9.0 0.2 edge.3
  9.2 3.2 %collective-permute-start.2 = (bf16[208,128]{1,0:T(8,128)(2,1)S(1)}, bf16[208,128]{1,0:T(8,128)(2,1)S(1)}, u32[]{:S(2)}, u32[]{:S(2)}) collective-permute-start(bf16[208,128]{1,0:T(8,128)(2,1)S(1)} %get-tuple-element.52), channel_id=1, source_target_pairs={{0,28},{4,0},{8,4},{12,8},{16,12},{20,16},{24,20},{28,24},{1,29},{... | collective-permute-start | bytes 159752 | tf_op jit(solution)/shard_map/ppermute | solution.py:33
  12.4 1.8 %inner.1 = (f32[24,64,128]{2,1,0:T(8,128)S(1)}, f32[4,64,128]{2,1,0:T(8,128)S(1)}, f32[24,128]{1,0:T(8,128)S(1)}) custom-call(f32[24,64,128]{2,1,0:T(8,128)S(1)} %get-tuple-element.39.air.air_low.air_high, bf16[2,24,64,128]{3,2,1,0:T(8,128)(2,1)S(1)} %get-tuple-element.40.winds.wind.wind_low.wind_high, bf16[64,192]{1,0:T(8,128)(2,1)S(1)} %get-tuple-element.55.stack_ref, ...), custom_call_target="tpu_custom_call" | custom-call | tf_op jit(solution)/shard_map/inner/pallas_call | solution.py:671
  14.2 0.3 %collective-permute-done.3.below_ref = bf16[208,128]{1,0:T(8,128)(2,1)S(1)} collective-permute-done((bf16[208,128]{1,0:T(8,128)(2,1)S(1)}, bf16[208,128]{1,0:T(8,128)(2,1)S(1)}, u32[]{:S(2)}, u32[]{:S(2)}) %collective-permute-start.3) | collective-permute-done | bytes 53280 | tf_op jit(solution)/shard_map/ppermute | solution.py:33
  14.5 0.0 collective-permute-done.2.above_ref
  14.5 0.9 %outer.1 = (f32[4,64,128]{2,1,0:T(8,128)S(1)}, f32[24,128]{1,0:T(8,128)S(1)}, f32[32,128]{1,0:T(8,128)S(1)}) custom-call(bf16[208,128]{1,0:T(8,128)(2,1)S(1)} %collective-permute-done.2.above_ref, bf16[208,128]{1,0:T(8,128)(2,1)S(1)} %collective-permute-done.3.below_ref, f32[2,64,128]{2,1,0:T(8,128)S(1)} %get-tuple-element.54.partial_low, ...), custom_call_target="tpu_custom_call" | custom-call | tf_op jit(solution)/shard_map/outer/pallas_call | solution.py:685
  15.4 0.9 %collective-permute-start.6 = (f32[32,128]{1,0:T(8,128)S(1)}, f32[32,128]{1,0:T(8,128)S(1)}, u32[]{:S(2)}, u32[]{:S(2)}) collective-permute-start(f32[32,128]{1,0:T(8,128)S(1)} %get-tuple-element.67.refs_0_), channel_id=1, source_target_pairs={{0,3},{1,0},{2,1},{3,2},{4,7},{5,4},{6,5},{7,6},{8,11},{9,8},{10,9... | collective-permute-start | bytes 49160 | tf_op jit(solution)/shard_map/ppermute | solution.py:33
  16.3 0.0 collective-permute-start.5
  16.4 1.1 %collective-permute-start.4 = (f32[32,128]{1,0:T(8,128)S(1)}, f32[32,128]{1,0:T(8,128)S(1)}, u32[]{:S(2)}, u32[]{:S(2)}) collective-permute-start(f32[32,128]{1,0:T(8,128)S(1)} %get-tuple-element.67.refs_0_), channel_id=1, source_target_pairs={{0,2},{1,3},{2,0},{3,1},{4,6},{5,7},{6,4},{7,5},{8,10},{9,11},{10,... | collective-permute-start | bytes 49160 | tf_op jit(solution)/shard_map/ppermute | solution.py:33
  17.5 0.9 %settle.1 = (f32[24,64,128]{2,1,0:T(8,128)}, f32[80,768]{1,0:T(8,128)S(1)}, f32[80,128]{1,0:T(8,128)S(1)}, f32[24,128]{1,0:T(8,128)S(1)}) custom-call(f32[4,64,128]{2,1,0:T(8,128)S(1)} %get-tuple-element.61.edges, f32[24,64,128]{2,1,0:T(8,128)S(1)} %get-tuple-element.62.inner, s32[1,24]{1,0:T(1,128)S(1)} %get-tuple-element.47.bank.refs_9_, ...), custom_call_target="tpu_custom_call" | custom-call | tf_op jit(solution)/shard_map/settle/pallas_call | solution.py:731
  18.4 0.0 collective-permute-done.6.refs_3_
  18.4 1.1 %collective-permute-done.5.refs_2_ = f32[32,128]{1,0:T(8,128)S(1)} collective-permute-done((f32[32,128]{1,0:T(8,128)S(1)}, f32[32,128]{1,0:T(8,128)S(1)}, u32[]{:S(2)}, u32[]{:S(2)}) %collective-permute-start.5) | collective-permute-done | bytes 16416 | tf_op jit(solution)/shard_map/ppermute | solution.py:33
  19.5 0.6 %collective-permute-done.4.refs_1_ = f32[32,128]{1,0:T(8,128)S(1)} collective-permute-done((f32[32,128]{1,0:T(8,128)S(1)}, f32[32,128]{1,0:T(8,128)S(1)}, u32[]{:S(2)}, u32[]{:S(2)}) %collective-permute-start.4) | collective-permute-done | bytes 16416 | tf_op jit(solution)/shard_map/ppermute | solution.py:33
  20.1 1.4 %last.1 = (f32[80,768]{1,0:T(8,128)}, f32[24,128]{1,0:T(8,128)}) custom-call(f32[32,128]{1,0:T(8,128)S(1)} %get-tuple-element.67.refs_0_, f32[32,128]{1,0:T(8,128)S(1)} %collective-permute-done.4.refs_1_, f32[32,128]{1,0:T(8,128)S(1)} %collective-permute-done.5.refs_2_, f32[32,128]{1,0:T(8,128)S(1)} %collective-permute-done.6.refs_3_, ...), custom_call_target="tpu_custom_call" | custom-call | tf_op jit(solution)/shard_map/last/pallas_call | solution.py:746
Async XLA Ops:
  2.5 4.7 %collective-permute-start = (bf16[64,128]{1,0:T(8,128)(2,1)S(1)}, bf16[64,128]{1,0:T(8,128)(2,1)S(1)}, u32[]{:S(2)}, u32[]{:S(2)}) collective-permute-start(bf16[64,128]{1,0:T(8,128)(2,1)S(1)} %get-tuple-element.41), channel_id=1, source_target_pairs={{0,1},{1,0},{2,3},{3,2},{4,5},{5,4},{6,7},{7,6},{8,9},{9,8},{10,11... | collective-permute-start | bytes 49160 | tf_op jit(solution)/shard_map/ppermute | solution.py:27
  3.0 4.2 %collective-permute-start.1 = (bf16[64,128]{1,0:T(8,128)(2,1)S(1)}, bf16[64,128]{1,0:T(8,128)(2,1)S(1)}, u32[]{:S(2)}, u32[]{:S(2)}) collective-permute-start(bf16[64,128]{1,0:T(8,128)(2,1)S(1)} %get-tuple-element.42), channel_id=1, source_target_pairs={{1,2},{3,0},{2,1},{0,3},{5,6},{7,4},{6,5},{4,7},{9,10},{11,8},{10,... | collective-permute-start | bytes 49160 | tf_op jit(solution)/shard_map/ppermute | solution.py:26
  7.4 7.1 %collective-permute-start.3 = (bf16[208,128]{1,0:T(8,128)(2,1)S(1)}, bf16[208,128]{1,0:T(8,128)(2,1)S(1)}, u32[]{:S(2)}, u32[]{:S(2)}) collective-permute-start(bf16[208,128]{1,0:T(8,128)(2,1)S(1)} %get-tuple-element.53), channel_id=1, source_target_pairs={{0,4},{4,8},{8,12},{12,16},{16,20},{20,24},{24,28},{28,0},{1,5},{5... | collective-permute-start | bytes 159752 | tf_op jit(solution)/shard_map/ppermute | solution.py:33
  9.2 5.3 %collective-permute-start.2 = (bf16[208,128]{1,0:T(8,128)(2,1)S(1)}, bf16[208,128]{1,0:T(8,128)(2,1)S(1)}, u32[]{:S(2)}, u32[]{:S(2)}) collective-permute-start(bf16[208,128]{1,0:T(8,128)(2,1)S(1)} %get-tuple-element.52), channel_id=1, source_target_pairs={{0,28},{4,0},{8,4},{12,8},{16,12},{20,16},{24,20},{28,24},{1,29},{... | collective-permute-start | bytes 159752 | tf_op jit(solution)/shard_map/ppermute | solution.py:33
  15.4 2.9 %collective-permute-start.6 = (f32[32,128]{1,0:T(8,128)S(1)}, f32[32,128]{1,0:T(8,128)S(1)}, u32[]{:S(2)}, u32[]{:S(2)}) collective-permute-start(f32[32,128]{1,0:T(8,128)S(1)} %get-tuple-element.67.refs_0_), channel_id=1, source_target_pairs={{0,3},{1,0},{2,1},{3,2},{4,7},{5,4},{6,5},{7,6},{8,11},{9,8},{10,9... | collective-permute-start | bytes 49160 | tf_op jit(solution)/shard_map/ppermute | solution.py:33
  16.3 3.2 %collective-permute-start.5 = (f32[32,128]{1,0:T(8,128)S(1)}, f32[32,128]{1,0:T(8,128)S(1)}, u32[]{:S(2)}, u32[]{:S(2)}) collective-permute-start(f32[32,128]{1,0:T(8,128)S(1)} %get-tuple-element.67.refs_0_), channel_id=1, source_target_pairs={{0,1},{1,2},{2,3},{3,0},{4,5},{5,6},{6,7},{7,4},{8,9},{9,10},{10,1... | collective-permute-start | bytes 49160 | tf_op jit(solution)/shard_map/ppermute | solution.py:33
  16.4 3.8 %collective-permute-start.4 = (f32[32,128]{1,0:T(8,128)S(1)}, f32[32,128]{1,0:T(8,128)S(1)}, u32[]{:S(2)}, u32[]{:S(2)}) collective-permute-start(f32[32,128]{1,0:T(8,128)S(1)} %get-tuple-element.67.refs_0_), channel_id=1, source_target_pairs={{0,2},{1,3},{2,0},{3,1},{4,6},{5,7},{6,4},{7,5},{8,10},{9,11},{10,... | collective-permute-start | bytes 49160 | tf_op jit(solution)/shard_map/ppermute | solution.py:33

commit v2 on v1

--- a/solution.py
+++ b/solution.py
@@ -72,14 +72,20 @@
     return field + physics_rate * jnp.tanh(tendency)
 
 
-def pack_kernel(air, wind, *refs):
-    others = (len(refs) - 7) // 2
-    packed, to_even, to_odd, air_here, wind_here = refs[others : others + 5]
-    sems, other_sems = refs[-2:]
+def pack_kernel(
+    air, wind, physics, mixing,
+    packed, to_even, to_odd, air_here, wind_here, physics_here, mixing_here, sems, square_sems,
+):
     rows, levels, width = air.shape
     lane = iota((levels, width), 1)
     place = lane // 4
     kind = lane % 4
+    squares = [
+        pltpu.make_async_copy(physics, physics_here, square_sems.at[0]),
+        pltpu.make_async_copy(mixing, mixing_here, square_sems.at[1]),
+    ]
+    for copy in squares:
+        copy.start()
     parts = sems.shape[1]
     size = rows // parts
     copies = []
@@ -93,12 +99,6 @@
         )
         for copy in copies[-1]:
             copy.start()
-    later = [
-        pltpu.make_async_copy(source, target, other_sems.at[at])
-        for at, (source, target) in enumerate(zip(refs[:others], refs[others + 5 : -2]))
-    ]
-    for copy in later:
-        copy.start()
     cells = jnp.zeros((levels, width), bf16)
     first = jnp.zeros((levels, width), bf16)
     second = jnp.zeros((levels, width), bf16)
@@ -118,7 +118,7 @@
     packed[...] = cells
     to_even[...] = pick(upper, to_high, to_low).astype(bf16)
     to_odd[...] = pick(upper, to_low, to_high).astype(bf16)
-    for copy in later:
+    for copy in squares:
         copy.wait()
 
 
@@ -274,64 +274,66 @@
     return fold(total, ocean_width)
 
 
-def start_kernel(
-    winds, shortwave, mask, route, tile, bank, physics, weights_far, ocean_far, mixing_far, _,
-    exchange_rate, message, forward, backward, stack, weights, ocean, mixing, sems,
-):
+def start_kernel(winds, physics, mixing, _, *refs):
+    count = 8
+    far, here = refs[:count], refs[count : 2 * count]
+    exchange_rate, message, wanted, forward, stack, sems = refs[2 * count :]
+    route, tile, mask, shortwave, bank, sea, weights, ocean = here
     copies = [
         pltpu.make_async_copy(source, target, sems.at[at])
-        for at, (source, target) in enumerate(
-            ((weights_far, weights), (ocean_far, ocean), (mixing_far, mixing))
-        )
+        for at, (source, target) in enumerate(zip(far, here))
     ]
     for copy in copies:
         copy.start()
-    stack[...] = physics_stack(physics[...])
-    for copy in copies:
-        copy.wait()
     rows, width = shortwave.shape
     banks, ocean_width, _ = weights.shape
-    flat = weights[...].reshape(banks * ocean_width, width)
-    high, low = split(flat)
-    backward[...] = jnp.concatenate([high, high, low], axis=0)
-    turned = flat.T
-    high, low = split(turned)
-    forward[...] = jnp.concatenate([high, high, low], axis=0)
-    frac = mask[...].astype(f32)
-    bank_at = as_column(bank[...].astype(f32)).astype(jnp.int32)
+    depth = ocean.shape[0]
+    lane = iota((rows, width), 1)
+    group = lax.axis_index("cpl")
     for x in range(rows):
         first = winds[0, x].astype(f32)[0:1]
         second = winds[1, x].astype(f32)[0:1]
         exchange_rate[x : x + 1] = first * first + second * second
+    level = iota((depth, width), 0)
+    profile = jnp.exp(level.astype(f32) / -8.0)
+    profile = profile / jnp.sum(profile, axis=0, keepdims=True)
+    unit = jnp.where(iota((depth, width), 1) == 0, (level == 0).astype(f32), profile)
+    message[...] = jnp.full(message.shape, -1.0, f32)
+    for copy in copies:
+        copy.wait()
+    stack[...] = physics_stack(physics[...])
+    frac = mask[...].astype(f32)
     exchange_rate[...] = frac * (0.5 + 2.0 * jnp.sqrt(exchange_rate[...] + 0.01))
+    target = route[...] * rows + tile[...]
+    target_at = as_column(target.astype(f32))
+    own_at = (group * rows + iota((rows, 1), 0)).astype(f32)
+    wanted[0:rows] = jnp.broadcast_to(target_at, (rows, width))
+    wanted[rows : 2 * rows] = jnp.broadcast_to(own_at, (rows, width))
+    for at in (0, 2 * ocean_width):
+        message[rows : rows + 1, at : at + rows] = target.astype(f32)
+        message[rows : rows + 1, at + ocean_width : at + ocean_width + rows] = (
+            group * rows + iota((1, rows), 1)
+        ).astype(f32)
+    bank_at = as_column(bank[...].astype(f32)).astype(jnp.int32)
+    high, low = split(weights[...].reshape(banks * ocean_width, width).T)
+    forward[...] = jnp.concatenate([high, high, low], axis=0)
     solar = chosen_shares(frac * shortwave[...], forward[...], bank_at, ocean_width)
-    lane = iota((rows, width), 1)
+    top = mixing[0:8]
     settled = 0.5 * ocean[0:8] + jnp.dot(
-        mixing[0:8], ocean[...], precision=highest, preferred_element_type=f32
-    )
-    group = lax.axis_index("cpl")
+        top, ocean[...], precision=highest, preferred_element_type=f32
+    )
+    answer = 0.5 * unit[0:8] + jnp.dot(top, unit, precision=highest, preferred_element_type=f32)
     surface = jnp.zeros((rows, width), f32)
     for at in range(0, rows * ocean_width, width):
         spread = jnp.broadcast_to(settled[0:1, at : at + width], (rows, width))
         surface = surface + jnp.where((lane + at) // ocean_width == iota((rows, width), 0), spread, 0.0)
     surface = fold(surface, ocean_width)
-    target = route[...] * rows + tile[...]
-    target_at = as_column(target.astype(f32))
-    own_at = (group * rows + iota((rows, width), 0)).astype(f32)
-    message[...] = jnp.full(message.shape, -1.0, f32)
     message[0:rows, :] = jnp.where(
         lane < 2 * ocean_width,
         solar,
-        jnp.where(
-            lane < 3 * ocean_width,
-            surface,
-            jnp.where(lane == 3 * ocean_width, target_at, own_at),
-        ),
-    )
-    message[rows : rows + 1, 0:rows] = target.astype(f32)
-    message[rows : rows + 1, ocean_width : ocean_width + rows] = (
-        group * rows + iota((1, rows), 1)
-    ).astype(f32)
+        jnp.where(lane < 3 * ocean_width, answer[0:1, 1:2] * solar, surface),
+    )
+    message[rows + 1 : rows + 2, :] = jnp.broadcast_to(answer[0:1, 0:1], (1, width))
 
 
 def make_outer_kernel(rows):
@@ -393,15 +395,23 @@
         bank_at = as_column(bank[...].astype(f32)).astype(jnp.int32)
         shares = chosen_shares(heat, forward[...], bank_at, ocean_width)
         message[...] = start[...]
+        lane = iota((rows, width), 1)
+        held = start[0:rows, :]
         message[0:rows, :] = jnp.where(
-            iota((rows, width), 1) < ocean_width, shares, start[0:rows, :]
+            lane < ocean_width,
+            shares,
+            jnp.where(
+                (lane >= 2 * ocean_width) & (lane < 3 * ocean_width),
+                held + start[rows + 1 : rows + 2, :] * shares,
+                held,
+            ),
         )
 
     return outer_kernel
 
 
 def settle_kernel(
-    edges, inner, bank, weights, ocean, mixing, out, base, response, total_weight, sems
+    edges, inner, bank, weights, ocean, mixing, out, base, response, total_weight, backward, sems
 ):
     rows = out.shape[0]
     middle = pl.ds(2, rows - 4)
@@ -415,6 +425,8 @@
     width = total_weight.shape[1]
     depth = ocean.shape[0]
     banks, ocean_width, _ = weights.shape
+    high, low = split(weights[...].reshape(banks * ocean_width, width))
+    backward[...] = jnp.concatenate([high, high, low], axis=0)
     sums = jnp.concatenate(
         [jnp.sum(weights[at], axis=0, keepdims=True) for at in range(banks)], axis=0
     )
@@ -436,7 +448,7 @@
 
 def make_last_kernel(count):
     def last_kernel(*refs):
-        messages, (base, response, total_weight, bottom, mask, bank, backward, ocean_next, surface, ocean_here, surface_here, sems) = (
+        messages, (wanted, base, response, total_weight, bottom, mask, bank, backward, ocean_next, surface, ocean_here, surface_here, sems) = (
             refs[:count],
             refs[count:],
         )
@@ -449,31 +461,18 @@
         slots = own.shape[0]
         ocean_width = slots
         cells = backward.shape[0] // 3
-        own_part = own[0:rows]
-        wanted = jnp.concatenate(
-            [
-                own_part[:, 3 * ocean_width : 3 * ocean_width + 1],
-                own_part[:, 3 * ocean_width + 1 : 3 * ocean_width + 2],
-            ],
-            axis=0,
-        )
-        top = response[0:1, 0:1]
-        sun = response[0:1, 1:2]
         lane = iota((slots, width), 1)
-        hot = []
+        labels = []
         values = []
         for block in blocks:
-            label = block[rows : rows + 1, 0 : 2 * ocean_width]
-            hot.append((wanted == label).astype(f32).astype(bf16))
-            raised = top * roll(block, 2 * ocean_width) + sun * roll(block, ocean_width)
-            values.append(
-                jnp.where(
-                    lane < 2 * ocean_width, block, jnp.where(lane < 3 * ocean_width, raised, 0.0)
-                )
-            )
-            values.append(
-                jnp.where((lane >= 2 * ocean_width) & (lane < 3 * ocean_width), block, 0.0)
-            )
+            labels.append(block[rows : rows + 1, :])
+            values.append(jnp.where(lane < 3 * ocean_width, block, 0.0))
+            values.append(jnp.where(lane < 3 * ocean_width, 0.0, block))
+        left = iota((1, width), 1) < 2 * ocean_width
+        hot = [
+            (wanted[...] == jnp.where(left, labels[at], labels[at + 1])).astype(f32).astype(bf16)
+            for at in range(0, len(labels), 2)
+        ]
         high, low = split(jnp.concatenate(values, axis=0))
         got = jnp.dot(
             jnp.concatenate(hot + hot, axis=1),
@@ -481,12 +480,7 @@
             preferred_element_type=f32,
         )
         near = iota((rows, width), 1)
-        seen = fold(
-            jnp.where(
-                (near >= 2 * ocean_width) & (near < 3 * ocean_width), got[0:rows], 0.0
-            ),
-            ocean_width,
-        )
+        seen = fold(jnp.where(near >= 2 * ocean_width, got[0:rows], 0.0), ocean_width)
         bank_at = as_column(bank[...].astype(f32)).astype(jnp.int32)
         high, low = split(
             jnp.concatenate(
@@ -561,85 +555,71 @@
     slots = ocean_width
     ocean_shape = ocean_temp.shape
 
-    others = (
-        physics,
-        sea_surface,
-        shortwave,
-        ocean_mask,
+    packed, to_even, to_odd, air_here, wind_here, physics, mixing = pl.pallas_call(
+        pack_kernel,
+        out_shape=(
+            pltpu.VMEM((levels, width), f32),
+            pltpu.VMEM((levels, width), bf16),
+            pltpu.VMEM((levels, width), bf16),
+            pltpu.VMEM(air_temp.shape, f32),
+            pltpu.VMEM(wind_field.shape, bf16),
+            pltpu.VMEM(physics.shape, f32),
+            pltpu.VMEM(mixing.shape, f32),
+        ),
+        in_specs=[pl.BlockSpec(memory_space=pltpu.HBM)] * 4,
+        out_specs=tuple(whole(7)),
+        scratch_shapes=[pltpu.SemaphoreType.DMA((2, 2)), pltpu.SemaphoreType.DMA((2,))],
+        compiler_params=params,
+        name="pack",
+    )(*(in_hbm(value) for value in (air_temp, wind_field, physics, mixing)))
+    even_side, odd_side = exchange(to_even, to_odd, "cpl")
+
+    far = (
         owner_route.reshape(1, rows),
         ocean_tile,
+        ocean_mask,
+        shortwave,
         weight_tile,
+        sea_surface,
+        remap_tiles,
+        ocean_temp,
     )
     (
-        packed,
-        to_even,
-        to_odd,
-        air_here,
-        wind_here,
-        physics,
+        _,
+        _,
+        ocean_mask,
+        shortwave,
+        weight_tile,
         sea_surface,
-        shortwave,
-        ocean_mask,
-        owner_route,
-        ocean_tile,
-        weight_tile,
-    ) = (
-        pl.pallas_call(
-            pack_kernel,
-            out_shape=(
-                pltpu.VMEM((levels, width), f32),
-                pltpu.VMEM((levels, width), bf16),
-                pltpu.VMEM((levels, width), bf16),
-            )
-            + tuple(
-                pltpu.VMEM(value.shape, value.dtype) for value in (air_temp, wind_field) + others
-            ),
-            in_specs=[pl.BlockSpec(memory_space=pltpu.HBM)] * (2 + len(others)),
-            out_specs=tuple(whole(5 + len(others))),
-            scratch_shapes=[
-                pltpu.SemaphoreType.DMA((2, 2)),
-                pltpu.SemaphoreType.DMA((len(others),)),
-            ],
-            compiler_params=params,
-            name="pack",
-        )(*(in_hbm(value) for value in (air_temp, wind_field) + others))
-    )
-    even_side, odd_side = exchange(to_even, to_odd, "cpl")
-
-    exchange_rate, start, forward, backward, stack, remap_tiles, ocean_temp, mixing = pl.pallas_call(
+        remap_tiles,
+        ocean_temp,
+        exchange_rate,
+        start,
+        wanted,
+        forward,
+        stack,
+    ) = pl.pallas_call(
         start_kernel,
         grid=(1,),
-        out_shape=(
+        out_shape=tuple(pltpu.VMEM(value.shape, value.dtype) for value in far)
+        + (
             shape_of((rows, width)),
             shape_of((slots, width)),
+            shape_of((2 * rows, width)),
             shape_of((3 * width, remap_tiles.shape[0] * ocean_width), bf16),
-            shape_of((3 * remap_tiles.shape[0] * ocean_width, width), bf16),
             shape_of((levels, 3 * levels), bf16),
-            pltpu.VMEM(remap_tiles.shape, f32),
-            pltpu.VMEM(ocean_shape, f32),
-            pltpu.VMEM(mixing.shape, f32),
         ),
-        in_specs=[pl.BlockSpec((2, rows, 16, width), lambda i: (0, 0, 0, 0))]
-        + whole(6)
-        + [pl.BlockSpec(memory_space=pltpu.HBM)] * 3
-        + [pl.BlockSpec(memory_space=pl.ANY)],
-        out_specs=whole(8),
-        scratch_shapes=[pltpu.SemaphoreType.DMA((3,))],
+        in_specs=[
+            pl.BlockSpec((2, rows, 16, width), lambda i: (0, 0, 0, 0)),
+            *whole(2),
+            pl.BlockSpec(memory_space=pl.ANY),
+        ]
+        + [pl.BlockSpec(memory_space=pltpu.HBM)] * len(far),
+        out_specs=whole(len(far) + 5),
+        scratch_shapes=[pltpu.SemaphoreType.DMA((len(far),))],
         compiler_params=params,
         name="start",
-    )(
-        wind_here,
-        shortwave,
-        ocean_mask,
-        owner_route,
-        ocean_tile,
-        weight_tile,
-        physics,
-        in_hbm(remap_tiles),
-        in_hbm(ocean_temp),
-        in_hbm(mixing),
-        packed,
-    )
+    )(wind_here, physics, mixing, packed, *(in_hbm(value) for value in far))
 
     last_pair = rows // 2 - 1
     air_specs = [
@@ -728,16 +708,17 @@
     else:
         gathered = [message, lax.all_gather(message, "cpl")]
 
-    air_next, base, response, total_weight = pl.pallas_call(
+    air_next, base, response, total_weight, backward = pl.pallas_call(
         settle_kernel,
         out_shape=(
             shape_of((rows, levels, width)),
             shape_of(ocean_shape),
             shape_of((ocean_shape[0], width)),
             shape_of((rows, width)),
+            shape_of((3 * remap_tiles.shape[0] * ocean_width, width), bf16),
         ),
         in_specs=whole(6),
-        out_specs=tuple([pl.BlockSpec(memory_space=pltpu.HBM)] + whole(3)),
+        out_specs=tuple([pl.BlockSpec(memory_space=pltpu.HBM)] + whole(4)),
         scratch_shapes=[pltpu.SemaphoreType.DMA((3,))],
         compiler_params=params,
         name="settle",
@@ -746,7 +727,7 @@
     ocean_next, surface_temp = pl.pallas_call(
         make_last_kernel(len(gathered)),
         out_shape=(shape_of(ocean_shape), shape_of((rows, width))),
-        in_specs=whole(len(gathered) + 7),
+        in_specs=whole(len(gathered) + 8),
         out_specs=(pl.BlockSpec(memory_space=pltpu.HBM),) * 2,
         scratch_shapes=[
             pltpu.VMEM(ocean_shape, f32),
@@ -757,6 +738,7 @@
         name="last",
     )(
         *gathered,
+        wanted,
         base,
         response,
         total_weight,

time: 21.7 us -> 21.3 us (0.982)
  starting transfers between devices: 9.98 us -> 9.61 us
    pallas_call x1, Pallas kernels: 1.57 us -> 1.96 us  [local(): pl.pallas_call(start_kernel, grid=(1,), out_shape=tuple((pltpu.VMEM(value...]
    ppermute x5, starting transfers between devices: 6.85 us -> 6.48 us  [shift(): lax.ppermute(block, axis, [(i, (i + turn) % count) for i in range(count)])]
    pallas_call x1, Pallas kernels: 1.38 us -> 1.12 us  [local(): pl.pallas_call(make_last_kernel(len(gathered)), out_shape=(shape_of(ocean...]
  transfers between devices with their start and end apart: 7 -> 7, of which waited for: 3 -> 4; matrix products, arithmetic and copies ran while one was open for 0% -> 0% of each run, Pallas kernels for 21% -> 23%
where the time goes in v2:
time: 21.3 us; the launch traced here: 21.1 us
  starting transfers between devices  9.61 us (45%)
  Pallas kernels  8.8 us (41%)
  waiting for transfers between devices  2.01 us (9%)
  between operations  0.7 us (3%)
    ppermute x5, starting transfers between devices, shift(): lax.ppermute(block, axis, [(i, (i + turn) % count) for i in range(count)])  6.48 us
    ppermute x1, starting transfers between devices, exchange(): odd_side = lax.ppermute(to_odd, axis, pair_odd(count))  2.61 us
    ppermute x5, waiting for transfers between devices, shift(): lax.ppermute(block, axis, [(i, (i + turn) % count) for i in range(count)])  2.01 us
    pallas_call x1, Pallas kernels, local(): pl.pallas_call(start_kernel, grid=(1,), out_shape=tuple((pltpu.VMEM(value...  1.96 us
    pallas_call x1, Pallas kernels, local(): pl.pallas_call(inner_kernel, out_shape=(pltpu.VMEM((rows, levels, width),...  1.8 us
    pallas_call x1, Pallas kernels, local(): pl.pallas_call(pack_kernel, out_shape=(pltpu.VMEM((levels, width), f32),...  1.76 us
    pallas_call x1, Pallas kernels, local(): pl.pallas_call(make_last_kernel(len(gathered)), out_shape=(shape_of(ocean...  1.12 us
    pallas_call x1, Pallas kernels, local(): pl.pallas_call(make_outer_kernel(rows), grid=(1,), out_shape=(shape_of((4...  0.91 us
  transfers between devices with their start and end apart: 7, of which 4 were waited for; matrix products, arithmetic and copies ran while one was open for 0% of the time, Pallas kernels for 23%

profile of v2, /device:TPU:0, one launch (start us, length us, event | category | flops | bytes accessed | tf_op | source)
XLA Modules:
  0.0 21.1 jit_solution(13987731932757841729)
XLA Ops:
  0.6 1.8 %pack.1 = (f32[64,128]{1,0:T(8,128)S(1)}, bf16[64,128]{1,0:T(8,128)(2,1)S(1)}, bf16[64,128]{1,0:T(8,128)(2,1)S(1)}, f32[24,64,128]{2,1,0:T(8,128)S(1)}, bf16[2,2...) custom-call(f32[24,64,128]{2,1,0:T(8,128)} %air.1, bf16[2,24,64,128]{3,2,1,0:T(8,128)(2,1)} %wind.1, ...), custom_call_target="tpu_custom_call" | custom-call | tf_op jit(solution)/shard_map/pack/pallas_call | solution.py:558
  2.4 0.5 %collective-permute-start = (bf16[64,128]{1,0:T(8,128)(2,1)S(1)}, bf16[64,128]{1,0:T(8,128)(2,1)S(1)}, u32[]{:S(2)}, u32[]{:S(2)}) collective-permute-start(bf16[64,128]{1,0:T(8,128)(2,1)S(1)} %get-tuple-element.39), channel_id=1, source_target_pairs={{0,1},{1,0},{2,3},{3,2},{4,5},{5,4},{6,7},{7,6},{8,9},{9,8},{10,11... | collective-permute-start | bytes 49160 | tf_op jit(solution)/shard_map/ppermute | solution.py:27
  2.9 2.6 %collective-permute-start.1 = (bf16[64,128]{1,0:T(8,128)(2,1)S(1)}, bf16[64,128]{1,0:T(8,128)(2,1)S(1)}, u32[]{:S(2)}, u32[]{:S(2)}) collective-permute-start(bf16[64,128]{1,0:T(8,128)(2,1)S(1)} %get-tuple-element.40), channel_id=1, source_target_pairs={{1,2},{3,0},{2,1},{0,3},{5,6},{7,4},{6,5},{4,7},{9,10},{11,8},{10,... | collective-permute-start | bytes 49160 | tf_op jit(solution)/shard_map/ppermute | solution.py:26
  5.5 2.0 %start.1 = (s32[1,24]{1,0:T(1,128)}, s32[1,24]{1,0:T(1,128)}, s32[24,128]{1,0:T(8,128)S(1)}, f32[24,128]{1,0:T(8,128)}, s32[1,24]{1,0:T(1,128)S(1)}, /*index=5*/...) custom-call(bf16[2,24,64,128]{3,2,1,0:T(8,128)(2,1)S(1)} %get-tuple-, ...), custom_call_target="tpu_custom_call" | custom-call | tf_op jit(solution)/shard_map/start/pallas_call | solution.py:601
  7.5 0.0 collective-permute-done.even_side
  7.5 0.0 collective-permute-done.1.odd_side
  7.5 0.2 edge.2
  7.7 1.6 %collective-permute-start.3 = (bf16[208,128]{1,0:T(8,128)(2,1)S(1)}, bf16[208,128]{1,0:T(8,128)(2,1)S(1)}, u32[]{:S(2)}, u32[]{:S(2)}) collective-permute-start(bf16[208,128]{1,0:T(8,128)(2,1)S(1)} %get-tuple-element.47), channel_id=1, source_target_pairs={{0,4},{4,8},{8,12},{12,16},{16,20},{20,24},{24,28},{28,0},{1,5},{5... | collective-permute-start | bytes 159752 | tf_op jit(solution)/shard_map/ppermute | solution.py:33
  9.3 0.2 edge.3
  9.4 3.3 %collective-permute-start.2 = (bf16[208,128]{1,0:T(8,128)(2,1)S(1)}, bf16[208,128]{1,0:T(8,128)(2,1)S(1)}, u32[]{:S(2)}, u32[]{:S(2)}) collective-permute-start(bf16[208,128]{1,0:T(8,128)(2,1)S(1)} %get-tuple-element.46), channel_id=1, source_target_pairs={{0,28},{4,0},{8,4},{12,8},{16,12},{20,16},{24,20},{28,24},{1,29},{... | collective-permute-start | bytes 159752 | tf_op jit(solution)/shard_map/ppermute | solution.py:33
  12.7 1.8 %inner.1 = (f32[24,64,128]{2,1,0:T(8,128)S(1)}, f32[4,64,128]{2,1,0:T(8,128)S(1)}, f32[24,128]{1,0:T(8,128)S(1)}) custom-call(f32[24,64,128]{2,1,0:T(8,128)S(1)} %get-tuple-element.37.air.air_low.air_high, bf16[2,24,64,128]{3,2,1,0:T(8,128)(2,1)S(1)} %get-tuple-element.38.winds.wind.wind_low.wind_high, bf16[64,192]{1,0:T(8,128)(2,1)S(1)} %get-tuple-element.49.stack_ref, ...), custom_call_target="tpu_custom_call" | custom-call | tf_op jit(solution)/shard_map/inner/pallas_call | solution.py:651
  14.5 0.1 collective-permute-done.3.below_ref
  14.6 0.1 collective-permute-done.2.above_ref
  14.8 0.9 %outer.1 = (f32[4,64,128]{2,1,0:T(8,128)S(1)}, f32[24,128]{1,0:T(8,128)S(1)}, f32[32,128]{1,0:T(8,128)S(1)}) custom-call(bf16[208,128]{1,0:T(8,128)(2,1)S(1)} %collective-permute-done.2.above_ref, bf16[208,128]{1,0:T(8,128)(2,1)S(1)} %collective-permute-done.3.below_ref, f32[2,64,128]{2,1,0:T(8,128)S(1)} %get-tuple-element.48.partial_low, ...), custom_call_target="tpu_custom_call" | custom-call | tf_op jit(solution)/shard_map/outer/pallas_call | solution.py:665
  15.7 0.5 %collective-permute-start.6 = (f32[32,128]{1,0:T(8,128)S(1)}, f32[32,128]{1,0:T(8,128)S(1)}, u32[]{:S(2)}, u32[]{:S(2)}) collective-permute-start(f32[32,128]{1,0:T(8,128)S(1)} %get-tuple-element.61.refs_0_), channel_id=1, source_target_pairs={{0,3},{1,0},{2,1},{3,2},{4,7},{5,4},{6,5},{7,6},{8,11},{9,8},{10,9... | collective-permute-start | bytes 49160 | tf_op jit(solution)/shard_map/ppermute | solution.py:33
  16.2 0.0 collective-permute-start.5
  16.2 1.1 %collective-permute-start.4 = (f32[32,128]{1,0:T(8,128)S(1)}, f32[32,128]{1,0:T(8,128)S(1)}, u32[]{:S(2)}, u32[]{:S(2)}) collective-permute-start(f32[32,128]{1,0:T(8,128)S(1)} %get-tuple-element.61.refs_0_), channel_id=1, source_target_pairs={{0,2},{1,3},{2,0},{3,1},{4,6},{5,7},{6,4},{7,5},{8,10},{9,11},{10,... | collective-permute-start | bytes 49160 | tf_op jit(solution)/shard_map/ppermute | solution.py:33
  17.3 0.9 %settle.1 = (f32[24,64,128]{2,1,0:T(8,128)}, f32[80,768]{1,0:T(8,128)S(1)}, f32[80,128]{1,0:T(8,128)S(1)}, f32[24,128]{1,0:T(8,128)S(1)}, bf16[1536,128]{1,0:T(8,128)(2,1)S(1)}) custom-call(f32[4,64,128]{2,1,0:T(8,128)S(1)} %get-tuple-element.56.edges, f32[24,64,128]{2,1,0:T(8,128)S(1)} %get-tuple-element.57.inner, ...), custom_call_target="tpu_custom_call" | custom-call | tf_op jit(solution)/shard_map/settle/pallas_call | solution.py:711
  18.2 0.0 collective-permute-done.6.refs_3_
  18.3 1.1 %collective-permute-done.5.refs_2_ = f32[32,128]{1,0:T(8,128)S(1)} collective-permute-done((f32[32,128]{1,0:T(8,128)S(1)}, f32[32,128]{1,0:T(8,128)S(1)}, u32[]{:S(2)}, u32[]{:S(2)}) %collective-permute-start.5) | collective-permute-done | bytes 16416 | tf_op jit(solution)/shard_map/ppermute | solution.py:33
  19.4 0.6 %collective-permute-done.4.refs_1_ = f32[32,128]{1,0:T(8,128)S(1)} collective-permute-done((f32[32,128]{1,0:T(8,128)S(1)}, f32[32,128]{1,0:T(8,128)S(1)}, u32[]{:S(2)}, u32[]{:S(2)}) %collective-permute-start.4) | collective-permute-done | bytes 16416 | tf_op jit(solution)/shard_map/ppermute | solution.py:33
  20.0 1.1 %last.1 = (f32[80,768]{1,0:T(8,128)}, f32[24,128]{1,0:T(8,128)}) custom-call(f32[32,128]{1,0:T(8,128)S(1)} %get-tuple-element.61.refs_0_, f32[32,128]{1,0:T(8,128)S(1)} %collective-permute-done.4.refs_1_, f32[32,128]{1,0:T(8,128)S(1)} %collective-permute-done.5.refs_2_, f32[32,128]{1,0:T(8,128)S(1)} %collective-permute-done.6.refs_3_, ...), custom_call_target="tpu_custom_call" | custom-call | tf_op jit(solution)/shard_map/last/pallas_call | solution.py:727
Async XLA Ops:
  2.4 5.1 %collective-permute-start = (bf16[64,128]{1,0:T(8,128)(2,1)S(1)}, bf16[64,128]{1,0:T(8,128)(2,1)S(1)}, u32[]{:S(2)}, u32[]{:S(2)}) collective-permute-start(bf16[64,128]{1,0:T(8,128)(2,1)S(1)} %get-tuple-element.39), channel_id=1, source_target_pairs={{0,1},{1,0},{2,3},{3,2},{4,5},{5,4},{6,7},{7,6},{8,9},{9,8},{10,11... | collective-permute-start | bytes 49160 | tf_op jit(solution)/shard_map/ppermute | solution.py:27
  2.9 4.6 %collective-permute-start.1 = (bf16[64,128]{1,0:T(8,128)(2,1)S(1)}, bf16[64,128]{1,0:T(8,128)(2,1)S(1)}, u32[]{:S(2)}, u32[]{:S(2)}) collective-permute-start(bf16[64,128]{1,0:T(8,128)(2,1)S(1)} %get-tuple-element.40), channel_id=1, source_target_pairs={{1,2},{3,0},{2,1},{0,3},{5,6},{7,4},{6,5},{4,7},{9,10},{11,8},{10,... | collective-permute-start | bytes 49160 | tf_op jit(solution)/shard_map/ppermute | solution.py:26
  7.7 6.9 %collective-permute-start.3 = (bf16[208,128]{1,0:T(8,128)(2,1)S(1)}, bf16[208,128]{1,0:T(8,128)(2,1)S(1)}, u32[]{:S(2)}, u32[]{:S(2)}) collective-permute-start(bf16[208,128]{1,0:T(8,128)(2,1)S(1)} %get-tuple-element.47), channel_id=1, source_target_pairs={{0,4},{4,8},{8,12},{12,16},{16,20},{20,24},{24,28},{28,0},{1,5},{5... | collective-permute-start | bytes 159752 | tf_op jit(solution)/shard_map/ppermute | solution.py:33
  9.4 5.3 %collective-permute-start.2 = (bf16[208,128]{1,0:T(8,128)(2,1)S(1)}, bf16[208,128]{1,0:T(8,128)(2,1)S(1)}, u32[]{:S(2)}, u32[]{:S(2)}) collective-permute-start(bf16[208,128]{1,0:T(8,128)(2,1)S(1)} %get-tuple-element.46), channel_id=1, source_target_pairs={{0,28},{4,0},{8,4},{12,8},{16,12},{20,16},{24,20},{28,24},{1,29},{... | collective-permute-start | bytes 159752 | tf_op jit(solution)/shard_map/ppermute | solution.py:33
  15.7 2.6 %collective-permute-start.6 = (f32[32,128]{1,0:T(8,128)S(1)}, f32[32,128]{1,0:T(8,128)S(1)}, u32[]{:S(2)}, u32[]{:S(2)}) collective-permute-start(f32[32,128]{1,0:T(8,128)S(1)} %get-tuple-element.61.refs_0_), channel_id=1, source_target_pairs={{0,3},{1,0},{2,1},{3,2},{4,7},{5,4},{6,5},{7,6},{8,11},{9,8},{10,9... | collective-permute-start | bytes 49160 | tf_op jit(solution)/shard_map/ppermute | solution.py:33
  16.2 3.2 %collective-permute-start.5 = (f32[32,128]{1,0:T(8,128)S(1)}, f32[32,128]{1,0:T(8,128)S(1)}, u32[]{:S(2)}, u32[]{:S(2)}) collective-permute-start(f32[32,128]{1,0:T(8,128)S(1)} %get-tuple-element.61.refs_0_), channel_id=1, source_target_pairs={{0,1},{1,2},{2,3},{3,0},{4,5},{5,6},{6,7},{7,4},{8,9},{9,10},{10,1... | collective-permute-start | bytes 49160 | tf_op jit(solution)/shard_map/ppermute | solution.py:33
  16.2 3.8 %collective-permute-start.4 = (f32[32,128]{1,0:T(8,128)S(1)}, f32[32,128]{1,0:T(8,128)S(1)}, u32[]{:S(2)}, u32[]{:S(2)}) collective-permute-start(f32[32,128]{1,0:T(8,128)S(1)} %get-tuple-element.61.refs_0_), channel_id=1, source_target_pairs={{0,2},{1,3},{2,0},{3,1},{4,6},{5,7},{6,4},{7,5},{8,10},{9,11},{10,... | collective-permute-start | bytes 49160 | tf_op jit(solution)/shard_map/ppermute | solution.py:33
